TPU v7x, 128 devices: a whole 4x4x4 slice. The times are simulated.
128 devices in a mesh: inline: 8 (over y, core), xline: 16 (over z, x).
Axes of the slice: x: 4, y: 4, z: 4, core: 2. Of those that a mesh axis runs over, the one named last changes fastest.
Arguments:
- records: bfloat16 [2, 8, 16, 8, 8192], P(None, 'inline', 'xline'), may hold values from -6 to 6
- beam_count: int32 [8, 16], P('inline', 'xline'), may hold values from 1 to 8, 80 in all within a row
- owner_list: int32 [10240, 1], P(('inline', 'xline')), may hold values from 0 to 15; in each aligned block of 80 rows (0 to 79, 80 to 159, ...) at most 10 rows name the same one
- block_list: int32 [10240, 1], P(('inline', 'xline')), may hold values from 0 to 127
- travel_table: float32 [2048, 64, 128], P('xline'), may hold values from 1 to 126
- amp_table: float32 [2048, 64, 128], P('xline'), may hold values from -6 to 6
Outputs:
- image: float32 [8, 16, 128], P('inline', 'xline')
Inputs may be any that keep to these rules, and one draw needn't show every extreme that they name: `owner_list`: the 80 rows of one tile name each owner at most 10 times, a bound that some block reaches. `beam_count`: some tile of every inline row has all 8 beams live.
All inputs are finite; a program needn't handle non-finite values. No bound on the sum of `beam_count` on one device may be relied on, other than what follows from the above.
Results may differ from a plain program's by a relative error of at most 0.0026.
Values may be sent and summed in bfloat16 or wider, within the bound.
A program may use at most 64 MiB of HBM per device.

v0:
```python
import jax
import jax.numpy as jnp
from jax import lax
from jax.sharding import PartitionSpec as P

NS = 128
NP = 64


def with_halo(value, sides, width):
    for axis, dim in sides:
        peers, length = (lax.axis_size(axis), value.shape[dim])
        up = [(i, (i + 1) % peers) for i in range(peers - 1)]
        down = [(j, i) for i, j in up]
        last = lax.slice_in_dim(value, length - width, length, axis=dim)
        leading = lax.slice_in_dim(value, 0, width, axis=dim)
        before = lax.ppermute(last, axis, up)
        after = lax.ppermute(leading, axis, down)
        value = jnp.concatenate([before, value, after], axis=dim)
    return value


def image_beam(record, travel, amplitude):
    samples = jnp.arange(NS, dtype=jnp.float32)
    weights = jnp.maximum(0.0, 1.0 - jnp.abs(samples[None, :, None] - travel[:, None, :])).astype(
        jnp.bfloat16
    )
    traces = jnp.einsum(
        "pt,ptx->px", record.reshape(NP, NS), weights, preferred_element_type=jnp.float32
    )
    contrib = jnp.sum(amplitude * traces, axis=0)
    energy = jnp.mean(jnp.square(record.astype(jnp.float32)))
    lighting = energy * jnp.sum(amplitude * amplitude, axis=0)
    return (contrib, lighting)


def per_device(records, beam_count, owner_list, block_list, travel_table, amp_table):
    beam_slots = records.shape[3]
    alive_mask = (jnp.arange(beam_slots, dtype=jnp.int32) < beam_count[0, 0]).astype(records.dtype)
    live_records = records * alive_mask[None, None, None, :, None]
    padded = with_halo(live_records, (("inline", 1), ("xline", 2)), 1)
    sources = jnp.stack(
        [padded[:, 1, 1], padded[:, 0, 1], padded[:, 2, 1], padded[:, 1, 0], padded[:, 1, 2]],
        axis=1,
    )
    requests = owner_list.shape[0]
    sources = sources.reshape(requests, NP * NS)
    owners = owner_list[:, 0]
    local_block = block_list[:, 0]
    members = lax.axis_size("xline")
    capacity = max(2, 2 * requests // members)
    matches = (owners[:, None] == jnp.arange(members, dtype=jnp.int32)[None, :]).astype(jnp.int32)
    slot_rank = jnp.sum((jnp.cumsum(matches, axis=0) - 1) * matches, axis=1)
    position = owners * capacity + slot_rank
    slot_blocks = (
        jnp.zeros((members * capacity,), jnp.int32)
        .at[position]
        .set(local_block)
        .reshape(members, capacity)
    )
    wanted = lax.all_to_all(slot_blocks, "xline", split_axis=0, concat_axis=0, tiled=True)
    travel_got = lax.all_to_all(
        travel_table[wanted], "xline", split_axis=0, concat_axis=0, tiled=True
    )
    amp_got = lax.all_to_all(amp_table[wanted], "xline", split_axis=0, concat_axis=0, tiled=True)
    travel_got = travel_got.reshape(members * capacity, NP, -1)[position]
    amp_got = amp_got.reshape(members * capacity, NP, -1)[position]

    def one_request(inputs):
        record, travel, amplitude = inputs
        return image_beam(record, travel, amplitude)

    contrib, lighting = lax.map(one_request, (sources, travel_got, amp_got), batch_size=4)
    summed = jnp.sum(contrib, axis=0)
    lighting_sum = jnp.sum(lighting, axis=0)
    return (summed / jnp.sqrt(1.0 + lighting_sum))[None, None, :]


def solution(mesh):
    placed = (
        P(None, "inline", "xline", None, None),
        P("inline", "xline"),
        P(("inline", "xline"), None),
        P(("inline", "xline"), None),
        P("xline", None, None),
        P("xline", None, None),
    )
    return jax.shard_map(
        per_device,
        mesh=mesh,
        in_specs=placed,
        out_specs=P("inline", "xline", None),
        check_vma=False,
    )
```

profile of v0, /device:TPU:1, one launch (start us, length us, event | category | flops | bytes accessed | tf_op | source)
XLA Modules:
  0.0 288.8 jit_solution(2905972682460500353)
XLA Ops:
  3.4 14.6 %all_to_all.22 = s32[16,1,10]{2,1,0:T(1,128)S(1)} all-to-all(s32[16,1,10]{2,1,0:T(1,128)S(1)} %bitcast.79), channel_id=1, replica_groups=mesh['inline'=8,'xline'=16] {'xline'}, dimensions={0} | all-to-all | bytes 1280 | tf_op jit(solution)/shard_map/all_to_all | solution.py:61
  18.1 5.5 %gather_fusion.2 = f32[160,64,128]{2,1,0:T(8,128)} fusion(f32[128,64,128]{2,1,0:T(8,128)} %param.12, s32[1024]{0:T(1024)S(1)} %pad_clamp_fusion.1), kind=kCustom, calls=%fused_computation.2 | custom fusion | bytes 10486400 | tf_op jit(solution)/shard_map/gather | solution.py:63
  23.6 4.7 %all-to-all-start.2 = ((f32[16,10,64,128]{3,2,1,0:T(8,128)}), f32[16,10,64,128]{3,2,1,0:T(8,128)}, u32[]{:S(2)}, u32[]{:S(2)}) async-start(f32[16,10,64,128]{3,2,1,0:T(8,128)} %bitcast.71), calls=%async_computation.2 | async-start | bytes 10485760 | tf_op jit(solution)/shard_map/all_to_all | solution.py:62
  29.1 5.2 %collective-permute-start = (bf16[2,1,1,8,8192]{4,3,0,2,1:T(8,128)(2,1)S(1)}, bf16[2,1,1,8,8192]{4,3,0,2,1:T(8,128)(2,1)S(1)}, u32[]{:S(2)}, u32[]{:S(2)}) collective-permute-start(bf16[2,1,1,8,8192]{4,3,0,2,1:T(8,128)(2,1)S(1)} %bitcast.77), channel_id=1, source_target_pairs={{0,16},{16,32},{32,48},{48,64},{64,80},{80,96},{96,112},{1,17},{17... | collective-permute-start | bytes 786440 | tf_op jit(solution)/shard_map/ppermute | solution.py:17
  36.3 5.4 %gather_fusion = f32[160,64,128]{2,1,0:T(8,128)} fusion(f32[128,64,128]{2,1,0:T(8,128)} %param.13, s32[1024]{0:T(1024)S(1)} %pad_clamp_fusion.1), kind=kCustom, calls=%fused_computation | custom fusion | bytes 10486400 | tf_op jit(solution)/shard_map/gather | solution.py:65
  43.8 4.9 %collective-permute-start.2 = (bf16[2,3,1,8,8192]{4,3,0,2,1:T(8,128)(2,1)S(1)}, bf16[2,3,1,8,8192]{4,3,0,2,1:T(8,128)(2,1)}, u32[]{:S(2)}, u32[]{:S(2)}) collective-permute-start(bf16[2,3,1,8,8192]{4,3,0,2,1:T(8,128)(2,1)S(1)} %copy.24), channel_id=1, source_target_pairs={{0,1},{1,2},{2,3},{3,4},{4,5},{5,6},{6,7},{7,8},{8,9},{9,10},{10,1... | collective-permute-start | bytes 2359304 | tf_op jit(solution)/shard_map/ppermute | solution.py:17
  48.8 57.1 %all-to-all-done.2 = f32[16,10,64,128]{3,2,1,0:T(8,128)} async-done(((f32[16,10,64,128]{3,2,1,0:T(8,128)}), f32[16,10,64,128]{3,2,1,0:T(8,128)}, u32[]{:S(2)}, u32[]{:S(2)}) %all-to-all-start.2) | async-done | bytes 5242912 | tf_op jit(solution)/shard_map/all_to_all | solution.py:62
  105.9 4.6 %all-to-all-start.1 = ((f32[16,10,64,128]{3,2,1,0:T(8,128)}), f32[16,10,64,128]{3,2,1,0:T(8,128)}, u32[]{:S(2)}, u32[]{:S(2)}) async-start(f32[16,10,64,128]{3,2,1,0:T(8,128)} %bitcast.70), calls=%async_computation.1 | async-start | bytes 10485760 | tf_op jit(solution)/shard_map/all_to_all | solution.py:65
  112.6 5.9 %collective-permute-done.3 = bf16[2,3,1,8,8192]{4,3,2,1,0:T(8,128)(2,1)} collective-permute-done((bf16[2,3,1,8,8192]{4,3,2,1,0:T(8,128)(2,1)S(1)}, bf16[2,3,1,8,8192]{4,3,2,1,0:T(8,128)(2,1)}, u32[]{:S(2)}, u32[]{:S(2)}) %collective-permute-start.3) | collective-permute-done | bytes 786464 | tf_op jit(solution)/shard_map/ppermute | solution.py:18
  121.0 3.2 %gather_fusion.3 = f32[80,64,128]{2,1,0:T(8,128)S(1)} fusion(f32[160,64,128]{2,1,0:T(8,128)} %bitcast.26, s32[1024]{0:T(1024)S(1)} %pad_clamp_fusion), kind=kCustom, calls=%fused_computation.3 | custom fusion | bytes 5243200 | tf_op jit(solution)/shard_map/gather | solution.py:66
  124.2 63.4 %all-to-all-done.1 = f32[16,10,64,128]{3,2,1,0:T(8,128)} async-done(((f32[16,10,64,128]{3,2,1,0:T(8,128)}), f32[16,10,64,128]{3,2,1,0:T(8,128)}, u32[]{:S(2)}, u32[]{:S(2)}) %all-to-all-start.1) | async-done | bytes 5242912 | tf_op jit(solution)/shard_map/all_to_all | solution.py:65
  187.6 4.7 %gather_fusion.1 = f32[80,64,128]{2,1,0:T(8,128)} fusion(f32[160,64,128]{2,1,0:T(8,128)} %bitcast.13, s32[1024]{0:T(1024)S(1)} %pad_clamp_fusion), kind=kCustom, calls=%fused_computation.1 | custom fusion | bytes 5243200 | tf_op jit(solution)/shard_map/gather | solution.py:67
  192.3 95.9 %while.12 = (s32[]{:T(128)}, f32[20,4,128]{2,1,0:T(4,128)S(1)}, f32[20,4,128]{2,1,0:T(4,128)S(1)}, f32[20,4,64,128]{3,2,1,0:T(8,128)}, bf16[20,4,8192]{2,1,0:T(4...) while((s32[]{:T(128)}, f32[20,4,128]{2,1,0:T(4,128)S(1)}, f32[20,4,128]{2,1,0:T(4,128)S(1)}, ...), condition=%wide.region_7.8_spmd, body=%wide.region_3.7_spmd.sunk | while | flops 29588992 | bytes 1127053 | solution.py:73
  198.2 2.6 fusion.18
  207.8 2.6 fusion.18
  217.4 2.6 fusion.18
  222.2 2.6 fusion.18
  227.0 2.6 fusion.18
  231.8 2.6 fusion.18
  236.6 2.6 fusion.18
  241.4 2.6 fusion.18
  246.2 2.6 fusion.18
  251.0 2.6 fusion.18
  255.8 2.6 fusion.18
  (161 shorter events, 79.6 us)
Async XLA Ops:
  23.6 5.4 %copy-start = (bf16[2,1,1,8,8192]{4,3,2,1,0:T(8,128)(2,1)S(1)}, bf16[2,1,1,8,8192]{4,3,2,1,0:T(8,128)(2,1)}, u32[]{:S(2)}) copy-start(bf16[2,1,1,8,8192]{4,3,2,1,0:T(8,128)(2,1)} %param.8) | copy-start | bytes 786436
  23.6 82.3 %all-to-all-start.2 = ((f32[16,10,64,128]{3,2,1,0:T(8,128)}), f32[16,10,64,128]{3,2,1,0:T(8,128)}, u32[]{:S(2)}, u32[]{:S(2)}) async-start(f32[16,10,64,128]{3,2,1,0:T(8,128)} %bitcast.71), calls=%async_computation.2 | async-start | bytes 10485760 | tf_op jit(solution)/shard_map/all_to_all | solution.py:62
  29.1 12.6 %collective-permute-start = (bf16[2,1,1,8,8192]{4,3,0,2,1:T(8,128)(2,1)S(1)}, bf16[2,1,1,8,8192]{4,3,0,2,1:T(8,128)(2,1)S(1)}, u32[]{:S(2)}, u32[]{:S(2)}) collective-permute-start(bf16[2,1,1,8,8192]{4,3,0,2,1:T(8,128)(2,1)S(1)} %bitcast.77), channel_id=1, source_target_pairs={{0,16},{16,32},{32,48},{48,64},{64,80},{80,96},{96,112},{1,17},{17... | collective-permute-start | bytes 786440 | tf_op jit(solution)/shard_map/ppermute | solution.py:17
  34.3 8.1 %collective-permute-start.1 = (bf16[2,1,1,8,8192]{4,3,0,2,1:T(8,128)(2,1)S(1)}, bf16[2,1,1,8,8192]{4,3,0,2,1:T(8,128)(2,1)S(1)}, u32[]{:S(2)}, u32[]{:S(2)}) collective-permute-start(bf16[2,1,1,8,8192]{4,3,0,2,1:T(8,128)(2,1)S(1)} %bitcast.78), channel_id=1, source_target_pairs={{16,0},{32,16},{48,32},{64,48},{80,64},{96,80},{112,96},{17,1},{33... | collective-permute-start | bytes 786440 | tf_op jit(solution)/shard_map/ppermute | solution.py:18
  42.5 76.0 %collective-permute-start.3 = (bf16[2,3,1,8,8192]{4,3,2,1,0:T(8,128)(2,1)S(1)}, bf16[2,3,1,8,8192]{4,3,2,1,0:T(8,128)(2,1)}, u32[]{:S(2)}, u32[]{:S(2)}) collective-permute-start(bf16[2,3,1,8,8192]{4,3,2,1,0:T(8,128)(2,1)S(1)} %pad_maximum_fusion), channel_id=1, source_target_pairs={{1,0},{2,1},{3,2},{4,3},{5,4},{6,5},{7,6},{8,7},{9,8},{10,9},{11,1... | collective-permute-start | bytes 2359304 | tf_op jit(solution)/shard_map/ppermute | solution.py:18
  43.8 67.8 %collective-permute-start.2 = (bf16[2,3,1,8,8192]{4,3,0,2,1:T(8,128)(2,1)S(1)}, bf16[2,3,1,8,8192]{4,3,0,2,1:T(8,128)(2,1)}, u32[]{:S(2)}, u32[]{:S(2)}) collective-permute-start(bf16[2,3,1,8,8192]{4,3,0,2,1:T(8,128)(2,1)S(1)} %copy.24), channel_id=1, source_target_pairs={{0,1},{1,2},{2,3},{3,4},{4,5},{5,6},{6,7},{7,8},{8,9},{9,10},{10,1... | collective-permute-start | bytes 2359304 | tf_op jit(solution)/shard_map/ppermute | solution.py:17
  105.9 81.7 %all-to-all-start.1 = ((f32[16,10,64,128]{3,2,1,0:T(8,128)}), f32[16,10,64,128]{3,2,1,0:T(8,128)}, u32[]{:S(2)}, u32[]{:S(2)}) async-start(f32[16,10,64,128]{3,2,1,0:T(8,128)} %bitcast.70), calls=%async_computation.1 | async-start | bytes 10485760 | tf_op jit(solution)/shard_map/all_to_all | solution.py:65
where the time goes:
time: 292 us; the launch traced here: 289 us
  waiting for transfers between devices  128 us (44%)
  matrix products  52 us (18%)
  other arithmetic  44.4 us (15%)
  local copies, waits for them, and re-layouts  25.6 us (9%)
  starting transfers between devices  22.6 us (8%)
  blocking collectives  14.6 us (5%)
    all_to_all x1, waiting for transfers between devices, per_device(): lax.all_to_all(amp_table[wanted], 'xline', split_axis=0, concat_axis=0, t...  63.4 us
    all_to_all x1, waiting for transfers between devices, per_device(): lax.all_to_all(travel_table[wanted], 'xline', split_axis=0, concat_axis=0...  57.1 us
    dot_general x20, matrix products, image_beam(): jnp.einsum('pt,ptx->px', record.reshape(NP, NS), weights, preferred_eleme...  52 us
    reduce_sum x20, other arithmetic, image_beam(): energy = jnp.mean(jnp.square(record.astype(jnp.float32)))  20.4 us
    reduce_sum x20, other arithmetic, image_beam(): lighting = energy * jnp.sum(amplitude * amplitude, axis=0)  19.1 us
    all_to_all x1, blocking collectives, per_device(): lax.all_to_all(slot_blocks, 'xline', split_axis=0, concat_axis=0, tiled=T...  14.6 us
    ppermute x2, starting transfers between devices, with_halo(): before = lax.ppermute(last, axis, up)  10.1 us
    ppermute x2, waiting for transfers between devices, with_halo(): after = lax.ppermute(leading, axis, down)  6.62 us
  transfers between devices with their start and end apart: 6, of which 5 were waited for; matrix products, arithmetic and copies ran while one was open for 4% of the time, Pallas kernels for 0%

commit v1 on v0

v1 whole, which is shorter than its diff:
```python
import jax
import jax.numpy as jnp
from jax import lax
from jax.experimental import pallas as pl
from jax.experimental.pallas import tpu as pltpu
from jax.sharding import PartitionSpec as P

NS = 128
NP = 64
BEAMS = 8
SHOTS = 2
RECS = SHOTS * BEAMS
COLS = 16
USES = 5 * RECS
LIST = 512
DEPTH = 8


def image_kernel(count, uses, energy, records, travel, amp, out, rec_buf, trav_buf, amp_buf, acc, sems):
    n = count[0]

    def copies(u):
        slot = lax.rem(u, DEPTH)
        word = uses[u]
        rec, block = word // 128 % 256, word % 128
        return (
            pltpu.make_async_copy(records.at[rec], rec_buf.at[slot], sems.at[slot, 0]),
            pltpu.make_async_copy(travel.at[block], trav_buf.at[slot], sems.at[slot, 1]),
            pltpu.make_async_copy(amp.at[block], amp_buf.at[slot], sems.at[slot, 2]),
        )

    def start(u):
        @pl.when(u < n)
        def _():
            for c in copies(u):
                c.start()

    for u in range(DEPTH - 1):
        start(jnp.int32(u))
    acc[...] = jnp.zeros_like(acc)

    def step(u, carry):
        start(u + DEPTH - 1)
        for c in copies(u):
            c.wait()
        slot = lax.rem(u, DEPTH)
        word = uses[u]
        rec, target = word // 128 % 256, word // (128 * 256)
        total = jnp.zeros((8, NS), jnp.float32)
        square = jnp.zeros((8, NS), jnp.float32)
        for q in range(NP // 8):
            rows = pl.ds(8 * q, 8)
            t = trav_buf[slot, rows, :]
            a = amp_buf[slot, rows, :]
            if q % 2 == 0:
                pair = rec_buf[slot, pl.ds(8 * q, 16), :].astype(jnp.float32)
            r = pair[8 * (q % 2) : 8 * (q % 2) + 8]
            k = t.astype(jnp.int32)
            f = t - k.astype(jnp.float32)
            w0 = (1.0 - f).astype(jnp.bfloat16).astype(jnp.float32)
            w1 = f.astype(jnp.bfloat16).astype(jnp.float32)
            v0 = jnp.take_along_axis(r, k, axis=1, mode="promise_in_bounds")
            v1 = jnp.take_along_axis(r, k + 1, axis=1, mode="promise_in_bounds")
            total += a * (v0 * w0 + v1 * w1)
            square += a * a
        acc[target, 0] += total
        acc[target, 1] += square * energy[rec]
        return carry

    lax.fori_loop(0, n, step, 0)
    out[...] = jnp.sum(acc[...], axis=2)


def image_uses(count, uses, energy, records, travel, amp):
    smem = pl.BlockSpec(memory_space=pltpu.SMEM)
    hbm = pl.BlockSpec(memory_space=pl.ANY)
    return pl.pallas_call(
        image_kernel,
        out_shape=jax.ShapeDtypeStruct((3 * COLS, 2, NS), jnp.float32),
        in_specs=[smem, smem, smem, hbm, hbm, hbm],
        out_specs=pl.BlockSpec(memory_space=pltpu.VMEM),
        scratch_shapes=[
            pltpu.VMEM((DEPTH, NP, NS), jnp.bfloat16),
            pltpu.VMEM((DEPTH, NP, NS), jnp.float32),
            pltpu.VMEM((DEPTH, NP, NS), jnp.float32),
            pltpu.VMEM((3 * COLS, 2, 8, NS), jnp.float32),
            pltpu.SemaphoreType.DMA((DEPTH, 3)),
        ],
        compiler_params=pltpu.CompilerParams(vmem_limit_bytes=16 << 20),
        cost_estimate=pl.CostEstimate(flops=10_000_000, bytes_accessed=8_000_000, transcendentals=0),
        name="image_uses",
    )(count, uses, energy, records, travel, amp)


def per_device(records, beam_count, owner_list, block_list, travel_table, amp_table):
    row, col = lax.axis_index("inline"), lax.axis_index("xline")
    rows = lax.axis_size("inline")
    up = [(i, i + 1) for i in range(rows - 1)]
    down = [(i + 1, i) for i in range(rows - 1)]
    records = records.reshape(RECS, NP, NS)
    gathered = lax.all_gather(records, "xline", axis=0, tiled=True)

    named = (owner_list * 128 + block_list)[:, 0].astype(jnp.float32)
    named = named.reshape(SHOTS, 5, BEAMS).transpose(1, 0, 2).reshape(5, RECS)
    from_next = lax.ppermute(named[1], "inline", down)
    from_prev = lax.ppermute(named[2], "inline", up)
    energy = jnp.mean(jnp.square(records.astype(jnp.float32)), axis=(1, 2))
    meta = jnp.concatenate(
        [
            named[0],
            from_next,
            from_prev,
            named[3],
            named[4],
            energy,
            jnp.full((32,), beam_count[0, 0].astype(jnp.float32)),
        ]
    )
    meta = lax.all_gather(meta, "xline", axis=0)
    names = meta[:, :USES].reshape(COLS, 5, SHOTS, BEAMS).astype(jnp.int32)
    energies = meta[:, USES : USES + RECS].reshape(COLS * RECS)
    counts = meta[:, USES + RECS].astype(jnp.int32)
    j = lax.broadcasted_iota(jnp.int32, names.shape, 0)
    k = lax.broadcasted_iota(jnp.int32, names.shape, 1)
    s = lax.broadcasted_iota(jnp.int32, names.shape, 2)
    b = lax.broadcasted_iota(jnp.int32, names.shape, 3)
    none = jnp.zeros((1,), jnp.int32)
    before = jnp.concatenate([none, counts[:-1]])
    after = jnp.concatenate([counts[1:], none])
    live = jnp.stack(
        [
            counts,
            jnp.where(row + 1 < rows, counts, 0),
            jnp.where(row > 0, counts, 0),
            before,
            after,
        ],
        axis=1,
    )
    wanted = (b < live[:, :, None, None]) & (names // 128 == col)
    source = j + (k == 4) - (k == 3)
    shift = 1 + (k == 1) - (k == 2)
    word = names % 128 + 128 * (source * RECS + s * BEAMS + b) + 128 * 256 * (shift * COLS + j)
    wanted, word = wanted.reshape(-1, NS), word.reshape(-1)
    marks = wanted.astype(jnp.float32)
    lanes = jnp.arange(NS)
    lines = jnp.arange(marks.shape[0])
    within = jnp.dot(marks, (lanes[:, None] <= lanes[None, :]).astype(jnp.float32))
    ahead = jnp.dot((lines[None, :] < lines[:, None]).astype(jnp.float32), within[:, -1:])
    place = jnp.where(wanted, (within + ahead).astype(jnp.int32) - 1, -1).reshape(-1)
    slots = jnp.arange(LIST, dtype=jnp.int32)
    uses = jnp.sum(jnp.where(place[None, :] == slots[:, None], word[None, :], 0), axis=1)
    count = jnp.sum(wanted.astype(jnp.int32)).reshape(1)

    sums = image_uses(count, uses, energies, gathered, travel_table, amp_table)
    sums = sums.reshape(3, COLS, 2 * NS)
    total = sums[1] + lax.ppermute(sums[0], "inline", down) + lax.ppermute(sums[2], "inline", up)
    mine = lax.psum_scatter(total, "xline", scatter_dimension=0, tiled=True)
    image = mine[0, :NS] / jnp.sqrt(1.0 + mine[0, NS:])
    return image[None, None, :]


def solution(mesh):
    placed = (
        P(None, "inline", "xline", None, None),
        P("inline", "xline"),
        P(("inline", "xline"), None),
        P(("inline", "xline"), None),
        P("xline", None, None),
        P("xline", None, None),
    )
    return jax.shard_map(
        per_device,
        mesh=mesh,
        in_specs=placed,
        out_specs=P("inline", "xline", None),
        check_vma=False,
    )
```

time: 292 us -> 181 us (0.62)
  the two profiles are of different devices: /device:TPU:1 before, /device:TPU:24 now
where the time goes in v1:
time: 181 us; the launch traced here: 180 us
  blocking collectives  100 us (55%)
  waiting for transfers between devices  24.2 us (13%)
  Pallas kernels  16.8 us (9%)
  between operations  14.2 us (8%)
  local copies, waits for them, and re-layouts  11.1 us (6%)
  starting transfers between devices  8.63 us (5%)
  other arithmetic  4.71 us (3%)
    unnamed x1, blocking collectives  78.6 us
    all_gather x1, waiting for transfers between devices, per_device(): gathered = lax.all_gather(records, 'xline', axis=0, tiled=True)  22.2 us
    all_gather x1, blocking collectives, per_device(): meta = lax.all_gather(meta, 'xline', axis=0)  21.9 us
    pallas_call x1, Pallas kernels, image_uses(): pl.pallas_call(image_kernel, out_shape=jax.ShapeDtypeStruct((3 * COLS, 2,...  16.8 us
    unnamed x12, local copies, waits for them, and re-layouts  8.92 us
  transfers between devices with their start and end apart: 5, of which 2 were waited for; matrix products, arithmetic and copies ran while one was open for 4% of the time, Pallas kernels for 0%

profile of v1, /device:TPU:24, one launch (start us, length us, event | category | flops | bytes accessed | tf_op | source)
XLA Modules:
  0.0 180.5 jit_solution(4644930343514903227)
XLA Ops:
  6.5 1.7 copy.37
  8.2 0.7 convert_reduce_fusion.1
  9.1 2.1 %collective-permute-start = (f32[16]{0:T(128)S(1)}, f32[16]{0:T(128)S(1)}, u32[]{:S(2)}, u32[]{:S(2)}) collective-permute-start(f32[16]{0:T(128)S(1)} %squeeze.30), channel_id=1, source_target_pairs={{16,0},{32,16},{48,32},{64,48},{80,64},{96,80},{112,96},{17,1},{33... | collective-permute-start | bytes 200 | tf_op jit(solution)/shard_map/ppermute | solution.py:105
  11.3 2.2 %collective-permute-start.1 = (f32[16]{0:T(128)S(1)}, f32[16]{0:T(128)S(1)}, u32[]{:S(2)}, u32[]{:S(2)}) collective-permute-start(f32[16]{0:T(128)S(1)} %squeeze.31), channel_id=1, source_target_pairs={{0,16},{16,32},{32,48},{48,64},{64,80},{80,96},{96,112},{1,17},{17... | collective-permute-start | bytes 200 | tf_op jit(solution)/shard_map/ppermute | solution.py:106
  13.8 1.1 multiply_reduce_fusion
  15.9 0.1 reshape.183
  16.1 0.1 reshape.176
  16.5 21.9 %all-gather.1 = f32[16,1,128]{2,1,0:T(1,128)S(1)} all-gather(f32[1,1,128]{2,1,0:T(1,128)S(1)} %bitcast.60), channel_id=2, replica_groups=mesh['inline'=8,'xline'=16] {'xline'}, dimensions={0}, use_global_device_ids=true | all-gather | bytes 8704 | tf_op jit(solution)/shard_map/all_gather | solution.py:119
  39.0 0.2 iota_compare_fusion.1
  39.4 0.7 convert_reduce_fusion
  40.2 0.1 fusion
  40.3 0.2 slice_reduce_fusion
  40.7 0.3 select_reduce_fusion.uses
  41.1 22.2 %all-gather.4.cloned.1.call-done.records = bf16[256,64,128]{2,1,0:T(8,128)(2,1)} async-done(((bf16[16,64,128]{2,1,0:T(8,128)(2,1)}), bf16[256,64,128]{2,1,0:T(8,128)(2,1)}) %all-gather.4.cloned.1.call-update) | async-done | bytes 4194320 | tf_op jit(solution)/shard_map/all_gather | solution.py:101
  63.3 2.2 %copy-done = f32[128,64,128]{2,1,0:T(8,128)S(1)} copy-done((f32[128,64,128]{2,1,0:T(8,128)S(1)}, f32[128,64,128]{2,1,0:T(8,128)}, u32[]{:S(2)}) %copy-start) | copy-done | bytes 4194328
  65.5 2.2 %copy-done.1 = f32[128,64,128]{2,1,0:T(8,128)S(1)} copy-done((f32[128,64,128]{2,1,0:T(8,128)S(1)}, f32[128,64,128]{2,1,0:T(8,128)}, u32[]{:S(2)}) %copy-start.1) | copy-done | bytes 4194328
  67.7 2.2 %copy-done.2 = bf16[256,64,128]{2,1,0:T(8,128)(2,1)S(1)} copy-done((bf16[256,64,128]{2,1,0:T(8,128)(2,1)S(1)}, bf16[256,64,128]{2,1,0:T(8,128)(2,1)}, u32[]{:S(2)}) %copy-start.2) | copy-done | bytes 4194328
  69.9 16.8 %image_uses.1 = f32[48,2,128]{2,1,0:T(2,128)S(1)} custom-call(s32[1]{0:T(128)} %bitcast.9.count, s32[512]{0:T(512)S(1)} %select_reduce_fusion.uses, f32[256]{0:T(256)S(1)} %reshape.172.energy, bf16[256,64,128]{2,1,0:T(8,128)(2,1)S(1)} %copy-done.2, f32[128,64,128]{2,1,0:T(8,128)S(1)} %copy-done, f32[128,64,128]{2,1,0:T(8,128)S(1)} %copy-done.1), custom_call_target="tpu_custom_call" | custom-call | flops 10000000 | bytes 8000000 | tf_op jit(solution)/shard_map/image_uses/pallas_call | solution.py:77
  86.7 1.9 %collective-permute-start.2 = (f32[16,256]{1,0:T(8,128)S(1)}, f32[16,256]{1,0:T(8,128)S(1)}, u32[]{:S(2)}, u32[]{:S(2)}) collective-permute-start(f32[16,256]{1,0:T(8,128)S(1)} %bitcast.58), channel_id=1, source_target_pairs={{16,0},{32,16},{48,32},{64,48},{80,64},{96,80},{112,96},{17,1},{33... | collective-permute-start | bytes 49160 | tf_op jit(solution)/shard_map/ppermute | solution.py:157
  88.7 2.4 %collective-permute-start.3 = (f32[16,256]{1,0:T(8,128)S(1)}, f32[16,256]{1,0:T(8,128)S(1)}, u32[]{:S(2)}, u32[]{:S(2)}) collective-permute-start(f32[16,256]{1,0:T(8,128)S(1)} %bitcast.59), channel_id=1, source_target_pairs={{0,16},{16,32},{32,48},{48,64},{64,80},{80,96},{96,112},{1,17},{17... | collective-permute-start | bytes 49160 | tf_op jit(solution)/shard_map/ppermute | solution.py:157
  91.1 0.7 dynamic-slice
  91.8 2.0 %collective-permute-done.3 = f32[16,256]{1,0:T(8,128)S(1)} collective-permute-done((f32[16,256]{1,0:T(8,128)S(1)}, f32[16,256]{1,0:T(8,128)S(1)}, u32[]{:S(2)}, u32[]{:S(2)}) %collective-permute-start.3) | collective-permute-done | bytes 16416 | tf_op jit(solution)/shard_map/ppermute | solution.py:157
  93.7 78.6 %all-reduce = f32[16,256]{1,0:T(8,128)S(1)} all-reduce(f32[16,256]{1,0:T(8,128)S(1)} %fusion.5), channel_id=3, replica_groups=mesh['inline'=8,'xline'=16] {'xline'}, use_global_device_ids=true, to_apply=%region_3.4.clone | all-reduce | flops 4096 | bytes 32768
  172.3 1.3 fusion.18
  (52 shorter events, 2.2 us)
Async XLA Ops:
  6.5 56.8 %all-gather.4.cloned.1.call-start = ((), (), s32[]{:S(2)}) async-start(), calls=%async_computation | async-start | bytes 4456448 | tf_op jit(solution)/shard_map/all_gather | solution.py:101
  9.1 7.2 %collective-permute-start = (f32[16]{0:T(128)S(1)}, f32[16]{0:T(128)S(1)}, u32[]{:S(2)}, u32[]{:S(2)}) collective-permute-start(f32[16]{0:T(128)S(1)} %squeeze.30), channel_id=1, source_target_pairs={{16,0},{32,16},{48,32},{64,48},{80,64},{96,80},{112,96},{17,1},{33... | collective-permute-start | bytes 200 | tf_op jit(solution)/shard_map/ppermute | solution.py:105
  11.3 5.1 %collective-permute-start.1 = (f32[16]{0:T(128)S(1)}, f32[16]{0:T(128)S(1)}, u32[]{:S(2)}, u32[]{:S(2)}) collective-permute-start(f32[16]{0:T(128)S(1)} %squeeze.31), channel_id=1, source_target_pairs={{0,16},{16,32},{32,48},{48,64},{64,80},{80,96},{96,112},{1,17},{17... | collective-permute-start | bytes 200 | tf_op jit(solution)/shard_map/ppermute | solution.py:106
  63.3 2.2 %copy-start = (f32[128,64,128]{2,1,0:T(8,128)S(1)}, f32[128,64,128]{2,1,0:T(8,128)}, u32[]{:S(2)}) copy-start(f32[128,64,128]{2,1,0:T(8,128)} %travel.1) | copy-start | bytes 12582916
  65.5 2.2 %copy-start.1 = (f32[128,64,128]{2,1,0:T(8,128)S(1)}, f32[128,64,128]{2,1,0:T(8,128)}, u32[]{:S(2)}) copy-start(f32[128,64,128]{2,1,0:T(8,128)} %amp.1) | copy-start | bytes 12582916
  67.7 2.2 %copy-start.2 = (bf16[256,64,128]{2,1,0:T(8,128)(2,1)S(1)}, bf16[256,64,128]{2,1,0:T(8,128)(2,1)}, u32[]{:S(2)}) copy-start(bf16[256,64,128]{2,1,0:T(8,128)(2,1)} %all-gather.4.cloned.1.call-done.records) | copy-start | bytes 12582916
  69.9 21.2 %copy-start.3 = (u32[128]{0:T(128)S(1)}, u32[128]{0:T(128)}, u32[]{:S(2)}) copy-start(u32[128]{0:T(128)} %constant.73) | copy-start | bytes 1540
  86.7 5.0 %collective-permute-start.2 = (f32[16,256]{1,0:T(8,128)S(1)}, f32[16,256]{1,0:T(8,128)S(1)}, u32[]{:S(2)}, u32[]{:S(2)}) collective-permute-start(f32[16,256]{1,0:T(8,128)S(1)} %bitcast.58), channel_id=1, source_target_pairs={{16,0},{32,16},{48,32},{64,48},{80,64},{96,80},{112,96},{17,1},{33... | collective-permute-start | bytes 49160 | tf_op jit(solution)/shard_map/ppermute | solution.py:157
  88.7 5.1 %collective-permute-start.3 = (f32[16,256]{1,0:T(8,128)S(1)}, f32[16,256]{1,0:T(8,128)S(1)}, u32[]{:S(2)}, u32[]{:S(2)}) collective-permute-start(f32[16,256]{1,0:T(8,128)S(1)} %bitcast.59), channel_id=1, source_target_pairs={{0,16},{16,32},{32,48},{48,64},{64,80},{80,96},{96,112},{1,17},{17... | collective-permute-start | bytes 49160 | tf_op jit(solution)/shard_map/ppermute | solution.py:157
Sparse Core Ops, SparseCore 0:
  9.5 53.7 all-gather.3

commit v2 on v0

v2 whole, which is shorter than its diff:
```python
import jax
import jax.numpy as jnp
from jax import lax
from jax.experimental import pallas as pl
from jax.experimental.pallas import tpu as pltpu
from jax.sharding import PartitionSpec as P

NS = 128
NP = 64
BEAMS = 8
SHOTS = 2
RECS = SHOTS * BEAMS
SIDE = 4
COLS = SIDE * SIDE
ROWS = 8
USES = 5 * RECS
LIST = 512
TARGETS = 3 * COLS
GROUP = 8
MESH = pl.DeviceIdType.MESH

ENERGY = USES
COUNT = USES + RECS


def greet(row, col):
    barrier = pltpu.get_barrier_semaphore()
    for other in range(1, COLS):
        pl.semaphore_signal(
            barrier, inc=1, device_id=(row, lax.rem(col + other, COLS)), device_id_type=MESH
        )

    @pl.when(row > 0)
    def _():
        pl.semaphore_signal(barrier, inc=1, device_id=(row - 1, col), device_id_type=MESH)

    @pl.when(row < ROWS - 1)
    def _():
        pl.semaphore_signal(barrier, inc=1, device_id=(row + 1, col), device_id_type=MESH)

    edges = (row > 0).astype(jnp.int32) + (row < ROWS - 1).astype(jnp.int32)
    pl.semaphore_wait(barrier, COLS - 1 + edges)


def gather_kernel(
    records, index, travel, amp,
    held, travel_out, amp_out, uses_out, index_out,
    near, mixed, lines, uses_vmem, index_vmem,
    local_sems, send_sems, recv_sems, near_send, near_recv, line_send, line_recv,
):
    row, col = lax.axis_index("inline"), lax.axis_index("xline")
    z, x = col // SIDE, lax.rem(col, SIDE)
    loads = [
        pltpu.make_async_copy(travel, travel_out, local_sems.at[0]),
        pltpu.make_async_copy(amp, amp_out, local_sems.at[1]),
        pltpu.make_async_copy(records, held.at[pl.ds(col * RECS, RECS)], local_sems.at[2]),
    ]
    near[...] = jnp.zeros_like(near)
    greet(row, col)

    def at(dz, dx):
        return lax.rem(z + dz + SIDE, SIDE) * SIDE + lax.rem(x + dx + SIDE, SIDE)

    started = {}

    def block(route, first, second, lo, size):
        tile = at(second, first) if route == 0 else at(first, second)
        return pl.ds(tile * RECS + route * BEAMS + lo, size)

    def toward(route, axis, step):
        along_x = (axis == 0) == (route == 0)
        return (row, at(0, step) if along_x else at(step, 0))

    def send(key, route, axis, step, first, second, lo, size):
        here = block(route, first, second, lo, size)
        n = len(started)
        if first == 0 and second == 0:
            source = records.at[pl.ds(route * BEAMS + lo, size)]
        else:
            source = held.at[here]
        copy = pltpu.make_async_remote_copy(
            src_ref=source,
            dst_ref=held.at[here],
            send_sem=send_sems.at[n],
            recv_sem=recv_sems.at[n],
            device_id=toward(route, axis, step),
            device_id_type=MESH,
        )
        copy.start()
        started[key] = copy

    half = BEAMS // 2
    both = (0, 1)
    for route in both:
        for step in (1, -1):
            send(("a", route, step), route, 0, step, 0, 0, 0, BEAMS)
    for route in both:
        for step in (1, -1):
            send(("c", route, 0, step), route, 1, step, 0, 0, 0, BEAMS)
    for copy in loads:
        copy.start()

    up = pltpu.make_async_remote_copy(
        index, near.at[0], near_send.at[0], near_recv.at[0], device_id=(row + 1, col), device_id_type=MESH
    )
    down = pltpu.make_async_remote_copy(
        index, near.at[1], near_send.at[1], near_recv.at[1], device_id=(row - 1, col), device_id_type=MESH
    )
    @pl.when(row < ROWS - 1)
    def _():
        up.start()

    @pl.when(row > 0)
    def _():
        down.start()

    @pl.when(row > 0)
    def _():
        up.wait_recv()

    @pl.when(row < ROWS - 1)
    def _():
        down.wait_recv()

    @pl.when(row < ROWS - 1)
    def _():
        up.wait_send()

    @pl.when(row > 0)
    def _():
        down.wait_send()

    kind = lax.broadcasted_iota(jnp.int32, (8, NS), 1) // RECS
    mixed[...] = jnp.where(kind == 1, near[1], jnp.where(kind == 2, near[0], index[...]))
    shares = []
    for other in range(1, COLS):
        share = pltpu.make_async_remote_copy(
            mixed,
            lines.at[other],
            line_send.at[other],
            line_recv.at[other],
            device_id=(row, lax.rem(col + other, COLS)),
            device_id_type=MESH,
        )
        share.start()
        shares.append(share)
    lines[0] = mixed[...]

    for route in both:
        for step in (1, -1):
            started["a", route, step].wait_recv()
            lo = 0 if step > 0 else half
            send(("b", route, step), route, 0, step, -step, 0, lo, half)
            for way in (1, -1):
                send(("c", route, -step, way), route, 1, way, -step, 0, 0, BEAMS)
    for route in both:
        for way in (1, -1):
            started["c", route, 0, way].wait_recv()
            lo = 0 if way > 0 else half
            send(("d", route, 0, way), route, 1, way, 0, -way, lo, half)

    build_list(row, col, shares, lines, index_vmem, uses_vmem)

    for route in both:
        for step in (1, -1):
            started["b", route, step].wait_recv()
        for way in (1, -1):
            send(("c", route, 2, way), route, 1, way, 2, 0, 0, BEAMS)
    for first in (-1, 1, 2):
        for route in both:
            for way in (1, -1):
                started["c", route, first, way].wait_recv()
                lo = 0 if way > 0 else half
                send(("d", route, first, way), route, 1, way, first, -way, lo, half)
    finish = [
        pltpu.make_async_copy(uses_vmem, uses_out, local_sems.at[3]),
        pltpu.make_async_copy(index_vmem, index_out, local_sems.at[4]),
    ]
    for copy in finish:
        copy.start()
    for first in (0, -1, 1, 2):
        for route in both:
            for way in (1, -1):
                started["d", route, first, way].wait_recv()
    for copy in started.values():
        copy.wait_send()
    for share in shares:
        share.wait_send()
    for copy in loads + finish:
        copy.wait()


def build_list(row, col, shares, lines, index_vmem, uses_vmem):
    for share in shares:
        share.wait_recv()
    for tile in range(COLS):
        index_vmem[pl.ds(tile, 1), :] = lines[lax.rem(col - tile + COLS, COLS)][0:1, :]
    table = index_vmem[...]
    names = table.astype(jnp.int32)
    shape = (COLS, NS)
    lane = lax.broadcasted_iota(jnp.int32, shape, 1)
    tile = lax.broadcasted_iota(jnp.int32, shape, 0)
    kind, beam = lane // RECS, lax.rem(lane, BEAMS)
    counts = jnp.broadcast_to(names[:, COUNT : COUNT + 1], shape)
    before = jnp.where(tile > 0, pltpu.roll(counts, 1, 0), 0)
    after = jnp.where(tile < COLS - 1, pltpu.roll(counts, COLS - 1, 0), 0)
    last, first = (row == ROWS - 1).astype(jnp.int32), (row == 0).astype(jnp.int32)
    live = jnp.where(kind == 3, before, jnp.where(kind == 4, after, counts))
    live = jnp.where(kind == 1, counts * (1 - last), live)
    live = jnp.where(kind == 2, counts * (1 - first), live)
    wanted = (lane < USES) & (beam < live) & (names // 128 == col)
    marks = wanted.astype(jnp.float32)
    earlier = lax.broadcasted_iota(jnp.int32, (NS, NS), 0) <= lax.broadcasted_iota(jnp.int32, (NS, NS), 1)
    within = jnp.dot(marks, earlier.astype(jnp.float32), preferred_element_type=jnp.float32)
    above = lax.broadcasted_iota(jnp.int32, (COLS, COLS), 1) < lax.broadcasted_iota(jnp.int32, (COLS, COLS), 0)
    totals = jnp.broadcast_to(jnp.sum(marks, axis=1, keepdims=True), shape)
    ahead = jnp.dot(above.astype(jnp.float32), totals, preferred_element_type=jnp.float32)
    place = jnp.where(wanted, within + ahead - 1.0, -1.0)
    number = jnp.sum(marks)

    source = tile + (kind == 4).astype(jnp.int32) - (kind == 3).astype(jnp.int32)
    shift = 1 + (kind == 1).astype(jnp.int32) - (kind == 2).astype(jnp.int32)
    fields = (
        lax.rem(names, 128).astype(jnp.float32),
        (source * RECS + lax.rem(lane, RECS)).astype(jnp.float32),
        (shift * COLS + tile).astype(jnp.float32),
    )
    upright = jnp.transpose(place)
    slot = lax.broadcasted_iota(jnp.int32, (NS, LIST), 1).astype(jnp.float32)
    line = lax.broadcasted_iota(jnp.int32, (8, NS), 0)
    listed = jnp.zeros((8, LIST), jnp.float32)
    for t in range(COLS):
        here = (jnp.broadcast_to(upright[:, t : t + 1], (NS, LIST)) == slot).astype(jnp.bfloat16)
        rows = jnp.zeros((8, NS), jnp.float32)
        for f, field in enumerate(fields):
            rows = jnp.where(line == f, jnp.broadcast_to(field[t : t + 1, :], (8, NS)), rows)
        listed += jnp.dot(rows.astype(jnp.bfloat16), here, preferred_element_type=jnp.float32)
    place_in = lax.broadcasted_iota(jnp.int32, (8, LIST), 1).astype(jnp.float32)
    part = lax.broadcasted_iota(jnp.int32, (8, LIST), 0)
    listed = jnp.where((part == 2) & (place_in >= number), float(TARGETS), listed)
    listed = jnp.where(part == 3, number, listed)
    uses_vmem[...] = listed.astype(jnp.int32)


def gather(records, index, travel, amp):
    hbm = pl.BlockSpec(memory_space=pl.ANY)
    vmem = pl.BlockSpec(memory_space=pltpu.VMEM)
    smem = pl.BlockSpec(memory_space=pltpu.SMEM)
    return pl.pallas_call(
        gather_kernel,
        out_shape=(
            pltpu.VMEM((COLS * RECS, NP, NS), jnp.bfloat16),
            pltpu.VMEM(travel.shape, jnp.float32),
            pltpu.VMEM(amp.shape, jnp.float32),
            jax.ShapeDtypeStruct((8, LIST), jnp.int32),
            jax.ShapeDtypeStruct((COLS, NS), jnp.float32),
        ),
        in_specs=[hbm, vmem, hbm, hbm],
        out_specs=(vmem, vmem, vmem, hbm, hbm),
        scratch_shapes=[
            pltpu.VMEM((2, 8, NS), jnp.float32),
            pltpu.VMEM((8, NS), jnp.float32),
            pltpu.VMEM((COLS, 8, NS), jnp.float32),
            pltpu.VMEM((8, LIST), jnp.int32),
            pltpu.VMEM((COLS, NS), jnp.float32),
            pltpu.SemaphoreType.DMA((5,)),
            pltpu.SemaphoreType.DMA((40,)),
            pltpu.SemaphoreType.DMA((40,)),
            pltpu.SemaphoreType.DMA((2,)),
            pltpu.SemaphoreType.DMA((2,)),
            pltpu.SemaphoreType.DMA((COLS,)),
            pltpu.SemaphoreType.DMA((COLS,)),
        ],
        compiler_params=pltpu.CompilerParams(
            collective_id=0, has_side_effects=True, vmem_limit_bytes=32 << 20
        ),
        cost_estimate=pl.CostEstimate(flops=10_000_000, bytes_accessed=16_000_000, transcendentals=0),
        name="gather_records",
    )(records, index, travel, amp)


def image_kernel(uses, index, records, travel, amp, out, acc):
    acc[...] = jnp.zeros_like(acc)

    def step(i, carry):
        picked = []
        for d in range(GROUP):
            u = i * GROUP + d
            picked.append((uses[0, u], uses[1, u], uses[2, u]))
        totals = [jnp.zeros((8, NS), jnp.float32) for _ in picked]
        squares = [jnp.zeros((8, NS), jnp.float32) for _ in picked]
        for q in range(NP // 8):
            rows = pl.ds(8 * q, 8)
            for d, (block, rec, _) in enumerate(picked):
                t = travel[block, rows, :]
                a = amp[block, rows, :]
                pair = records[rec, pl.ds(16 * (q // 2), 16), :].astype(jnp.float32)
                r = pair[8 * (q % 2) : 8 * (q % 2) + 8]
                k = t.astype(jnp.int32)
                f = t - k.astype(jnp.float32)
                w0 = (1.0 - f).astype(jnp.bfloat16).astype(jnp.float32)
                w1 = f.astype(jnp.bfloat16).astype(jnp.float32)
                v0 = jnp.take_along_axis(r, k, axis=1, mode="promise_in_bounds")
                v1 = jnp.take_along_axis(r, k + 1, axis=1, mode="promise_in_bounds")
                totals[d] += a * (v0 * w0 + v1 * w1)
                squares[d] += a * a
        for d, (_, rec, target) in enumerate(picked):
            energy = index[rec // RECS, ENERGY + lax.rem(rec, RECS)]
            acc[target, 0] += totals[d]
            acc[target, 1] += squares[d] * energy
        return carry

    lax.fori_loop(0, (uses[3, 0] + GROUP - 1) // GROUP, step, 0)
    out[...] = jnp.sum(acc[pl.ds(0, TARGETS)], axis=2)


def image(uses, index, records, travel, amp):
    vmem = pl.BlockSpec(memory_space=pltpu.VMEM)
    smem = pl.BlockSpec(memory_space=pltpu.SMEM)
    return pl.pallas_call(
        image_kernel,
        out_shape=pltpu.VMEM((TARGETS, 2, NS), jnp.float32),
        in_specs=[smem, smem, vmem, vmem, vmem],
        out_specs=vmem,
        scratch_shapes=[pltpu.VMEM((TARGETS + 1, 2, 8, NS), jnp.float32)],
        compiler_params=pltpu.CompilerParams(vmem_limit_bytes=32 << 20),
        cost_estimate=pl.CostEstimate(flops=10_000_000, bytes_accessed=8_000_000, transcendentals=0),
        name="image_uses",
    )(uses, index, records, travel, amp)


def exchange_kernel(sums, out, near, total, parts, near_send, near_recv, part_send, part_recv):
    row, col = lax.axis_index("inline"), lax.axis_index("xline")
    greet(row, col)
    up = pltpu.make_async_remote_copy(
        sums.at[2], near.at[0], near_send.at[0], near_recv.at[0], device_id=(row + 1, col), device_id_type=MESH
    )
    down = pltpu.make_async_remote_copy(
        sums.at[0], near.at[1], near_send.at[1], near_recv.at[1], device_id=(row - 1, col), device_id_type=MESH
    )

    @pl.when(row < ROWS - 1)
    def _():
        up.start()

    @pl.when(row > 0)
    def _():
        down.start()

    total[...] = sums[1]

    @pl.when(row > 0)
    def _():
        up.wait_recv()
        total[...] += near[0]

    @pl.when(row < ROWS - 1)
    def _():
        down.wait_recv()
        total[...] += near[1]

    copies = []
    for other in range(1, COLS):
        there = lax.rem(col + other, COLS)
        copy = pltpu.make_async_remote_copy(
            total.at[there],
            parts.at[other],
            part_send.at[other],
            part_recv.at[other],
            device_id=(row, there),
            device_id_type=MESH,
        )
        copy.start()
        copies.append(copy)
    mine = total[col]
    for copy, other in zip(copies, range(1, COLS)):
        copy.wait_recv()
        mine += parts[other]
    out[0] = mine[0:1] / jnp.sqrt(1.0 + mine[1:2])
    for copy in copies:
        copy.wait_send()

    @pl.when(row < ROWS - 1)
    def _():
        up.wait_send()

    @pl.when(row > 0)
    def _():
        down.wait_send()


def exchange(sums):
    vmem = pl.BlockSpec(memory_space=pltpu.VMEM)
    return pl.pallas_call(
        exchange_kernel,
        out_shape=jax.ShapeDtypeStruct((1, 1, NS), jnp.float32),
        in_specs=[vmem],
        out_specs=vmem,
        scratch_shapes=[
            pltpu.VMEM((2, COLS, 2, NS), jnp.float32),
            pltpu.VMEM((COLS, 2, NS), jnp.float32),
            pltpu.VMEM((COLS, 2, NS), jnp.float32),
            pltpu.SemaphoreType.DMA((2,)),
            pltpu.SemaphoreType.DMA((2,)),
            pltpu.SemaphoreType.DMA((COLS,)),
            pltpu.SemaphoreType.DMA((COLS,)),
        ],
        compiler_params=pltpu.CompilerParams(collective_id=1, has_side_effects=True),
        cost_estimate=pl.CostEstimate(flops=10_000, bytes_accessed=100_000, transcendentals=0),
        name="exchange_sums",
    )(sums)


def per_device(records, beam_count, owner_list, block_list, travel_table, amp_table):
    records = records.reshape(RECS, NP, NS)
    named = (owner_list * 128 + block_list)[:, 0].astype(jnp.float32)
    named = named.reshape(SHOTS, 5, BEAMS).transpose(1, 0, 2).reshape(USES)
    energy = jnp.mean(jnp.square(records.astype(jnp.float32)), axis=(1, 2))
    count = jnp.broadcast_to(beam_count[0].astype(jnp.float32), (NS - COUNT,))
    index = jnp.broadcast_to(jnp.concatenate([named, energy, count]), (8, NS))
    gathered, travel, amp, uses, index = gather(records, index, travel_table, amp_table)
    sums = image(uses, index, gathered, travel, amp)
    return exchange(sums.reshape(3, COLS, 2, NS))


def solution(mesh):
    placed = (
        P(None, "inline", "xline", None, None),
        P("inline", "xline"),
        P(("inline", "xline"), None),
        P(("inline", "xline"), None),
        P("xline", None, None),
        P("xline", None, None),
    )
    return jax.shard_map(
        per_device,
        mesh=mesh,
        in_specs=placed,
        out_specs=P("inline", "xline", None),
        check_vma=False,
    )
```

time: 292 us -> 62.6 us (0.21)
  waiting for transfers between devices: 128 us -> 0 us
  Pallas kernels: 0 us -> 52.3 us
  matrix products: 52 us -> 0 us
  other arithmetic: 44.4 us -> 1.89 us
  starting transfers between devices: 22.6 us -> 0 us
  local copies, waits for them, and re-layouts: 25.6 us -> 7.43 us
  blocking collectives: 14.6 us -> 0 us
    all_to_all x2 -> x0, waiting for transfers between devices: 121 us -> none  [the longest x1 63.4 us: per_device(): lax.all_to_all(amp_table[wanted], 'xline', split_axis=0, concat_axis=0, t...]
    pallas_call x0 -> x3, Pallas kernels: none -> 52.3 us  [the longest x1 31.4 us: gather(): pl.pallas_call(gather_kernel, out_shape=(pltpu.VMEM((COLS * RECS, NP, NS)...]
    dot_general x20 -> x0, matrix products: 52 us -> none  [image_beam(): jnp.einsum('pt,ptx->px', record.reshape(NP, NS), weights, preferred_eleme...]
    reduce_sum x43 -> x1, other arithmetic: 40.4 us -> 1.11 us  [per_device(): energy = jnp.mean(jnp.square(records.astype(jnp.float32)), axis=(1, 2))]
    gather x4 -> x0, local copies, waits for them, and re-layouts: 18.8 us -> none  [the longest x1 5.45 us: per_device(): travel_table[wanted]]
    all_to_all x1 -> x0, blocking collectives: 14.6 us -> none  [per_device(): lax.all_to_all(slot_blocks, 'xline', split_axis=0, concat_axis=0, tiled=T...]
    ppermute x4 -> x0, starting transfers between devices: 13.3 us -> none  [the longest x2 10.1 us: with_halo(): before = lax.ppermute(last, axis, up)]
    all_to_all x2 -> x0, starting transfers between devices: 9.3 us -> none  [the longest x1 4.7 us: per_device(): lax.all_to_all(travel_table[wanted], 'xline', split_axis=0, concat_axis=0...]
  transfers between devices with their start and end apart: 6 -> 0, of which waited for: 5 -> 0; matrix products, arithmetic and copies ran while one was open for 4% -> 0% of each run, Pallas kernels for 0% -> 0%
where the time goes in v2:
time: 62.6 us; the launch traced here: 62.3 us
  Pallas kernels  52.3 us (84%)
  local copies, waits for them, and re-layouts  7.43 us (12%)
  other arithmetic  1.89 us (3%)
  between operations  0.71 us (1%)
    pallas_call x1, Pallas kernels, gather(): pl.pallas_call(gather_kernel, out_shape=(pltpu.VMEM((COLS * RECS, NP, NS)...  31.4 us
    pallas_call x1, Pallas kernels, exchange(): pl.pallas_call(exchange_kernel, out_shape=jax.ShapeDtypeStruct((1, 1, NS)...  17.6 us
    unnamed x8, local copies, waits for them, and re-layouts  7.16 us
    pallas_call x1, Pallas kernels, image(): pl.pallas_call(image_kernel, out_shape=pltpu.VMEM((TARGETS, 2, NS), jnp.f...  3.26 us

profile of v2, /device:TPU:1, one launch (start us, length us, event | category | flops | bytes accessed | tf_op | source)
XLA Modules:
  0.0 62.3 jit_solution(5174326077554543569)
XLA Ops:
  0.7 0.7 %convert_reduce_fusion = f32[80]{0:T(128)S(1)} fusion(s32[80,1]{0,1:T(1,128)} %param.9, s32[80,1]{0,1:T(1,128)} %param.8), kind=kLoop, calls=%fused_computation.3 | loop fusion | flops 240 | bytes 960 | tf_op jit(solution)/shard_map/convert_element_type | solution.py:416
  1.4 1.1 %multiply_reduce_fusion = f32[2,8]{1,0:T(2,128)S(1)} fusion(bf16[2,1,1,8,8192]{4,3,2,1,0:T(8,128)(2,1)} %param.6), kind=kLoop, calls=%fused_computation | loop fusion | flops 393200 | bytes 262208 | tf_op jit(solution)/shard_map/reduce_sum | solution.py:418
  2.5 0.1 div.6
  2.6 0.1 convert_element_type.16
  2.6 0.1 reshape.20
  2.7 0.1 pad_maximum_fusion
  2.8 1.0 %copy.9 = bf16[2,8,64,128]{3,2,1,0:T(8,128)(2,1)S(1)} copy(bf16[2,8,64,128]{3,1,2,0:T(8,128)(2,1)} %bitcast.9) | data formatting | bytes 524288
  3.8 0.0 copy-start
  3.8 2.2 %copy-done = f32[128,64,128]{2,1,0:T(8,128)S(1)} copy-done((f32[128,64,128]{2,1,0:T(8,128)S(1)}, f32[128,64,128]{2,1,0:T(8,128)}, u32[]{:S(2)}) %copy-start) | copy-done | bytes 4194328
  6.0 0.0 copy-start.1
  6.0 2.2 %copy-done.1 = f32[128,64,128]{2,1,0:T(8,128)S(1)} copy-done((f32[128,64,128]{2,1,0:T(8,128)S(1)}, f32[128,64,128]{2,1,0:T(8,128)}, u32[]{:S(2)}) %copy-start.1) | copy-done | bytes 4194328
  8.2 31.4 %gather_records.1 = (bf16[256,64,128]{2,1,0:T(8,128)(2,1)S(1)}, f32[128,64,128]{2,1,0:T(8,128)S(1)}, f32[128,64,128]{2,1,0:T(8,128)S(1)}, s32[8,512]{1,0:T(8,128)S(1)}, f32[16,128]{1,0:T(8,128)S(1)}) custom-call(bf16[16,64,128]{2,1,0:T(8,128)(2,1)S(1)} %bitcast.7, f32[8,128]{1,0:T(8,128)S(1)} %broadcast_in_dim.12.index, f32[128,64,128]{2,1,0:T(8,128)S(1)} %copy-done, ...), custom_call_target="tpu_custom_call" | custom-call | flops 10000000 | bytes 16000000 | tf_op jit(solution)/shard_map/gather_records/pallas_call | solution.py:249
  39.6 3.3 %image_uses.1 = f32[48,2,128]{2,1,0:T(2,128)S(1)} custom-call(s32[8,512]{1,0:T(8,128)S(1)} %get-tuple-element.10.uses, f32[16,128]{1,0:T(8,128)S(1)} %get-tuple-element.11.index, bf16[256,64,128]{2,1,0:T(8,128)(2,1)S(1)} %get-tuple-element.12.records, f32[128,64,128]{2,1,0:T(8,128)S(1)} %get-tuple-element.13.travel, f32[128,64,128]{2,1,0:T(8,128)S(1)} %get-tuple-element.14.amp), custom_call_target="tpu_custom_call" | custom-call | flops 10000000 | bytes 8000000 | tf_op jit(solution)/shard_map/image_uses/pallas_call | solution.py:320
  42.8 0.0 copy-start.2
  42.8 0.6 copy-done.2
  43.5 17.6 %exchange_sums.1 = f32[1,1,128]{2,1,0:T(1,128)} custom-call(f32[3,16,2,128]{3,2,1,0:T(2,128)} %bitcast.8), custom_call_target="tpu_custom_call" | custom-call | flops 10000 | bytes 100000 | tf_op jit(solution)/shard_map/exchange_sums/pallas_call | solution.py:394
  61.1 1.2 %copy.12 = f32[1,1,128]{2,1,0:T(1,128)} copy(f32[1,1,128]{2,1,0:T(1,128)} %exchange_sums.1) | data formatting | bytes 1024
  (4 shorter events, 0.0 us)
Async XLA Ops:
  3.8 2.2 %copy-start = (f32[128,64,128]{2,1,0:T(8,128)S(1)}, f32[128,64,128]{2,1,0:T(8,128)}, u32[]{:S(2)}) copy-start(f32[128,64,128]{2,1,0:T(8,128)} %travel.1) | copy-start | bytes 12582916
  6.0 2.2 %copy-start.1 = (f32[128,64,128]{2,1,0:T(8,128)S(1)}, f32[128,64,128]{2,1,0:T(8,128)}, u32[]{:S(2)}) copy-start(f32[128,64,128]{2,1,0:T(8,128)} %amp.1) | copy-start | bytes 12582916
  42.8 0.6 copy-start.2

commit v3 on v2

--- a/solution.py
+++ b/solution.py
@@ -418,6 +418,8 @@
     energy = jnp.mean(jnp.square(records.astype(jnp.float32)), axis=(1, 2))
     count = jnp.broadcast_to(beam_count[0].astype(jnp.float32), (NS - COUNT,))
     index = jnp.broadcast_to(jnp.concatenate([named, energy, count]), (8, NS))
+    travel_table = pltpu.with_memory_space_constraint(travel_table, pltpu.HBM)
+    amp_table = pltpu.with_memory_space_constraint(amp_table, pltpu.HBM)
     gathered, travel, amp, uses, index = gather(records, index, travel_table, amp_table)
     sums = image(uses, index, gathered, travel, amp)
     return exchange(sums.reshape(3, COLS, 2, NS))

time: 62.6 us -> 56.7 us (0.906)
  local copies, waits for them, and re-layouts: 7.43 us -> 3.06 us
  Pallas kernels: 52.3 us -> 50.5 us
    unnamed x8 -> x4, local copies, waits for them, and re-layouts: 7.16 us -> 2.79 us
    pallas_call x1, Pallas kernels: 17.6 us -> 15.2 us  [exchange(): pl.pallas_call(exchange_kernel, out_shape=jax.ShapeDtypeStruct((1, 1, NS)...]
where the time goes in v3:
time: 56.7 us; the launch traced here: 56.1 us
  Pallas kernels  50.5 us (89%)
  local copies, waits for them, and re-layouts  3.06 us (5%)
  other arithmetic  1.89 us (3%)
  between operations  0.7 us (1%)
    pallas_call x1, Pallas kernels, gather(): pl.pallas_call(gather_kernel, out_shape=(pltpu.VMEM((COLS * RECS, NP, NS)...  31.5 us
    pallas_call x1, Pallas kernels, exchange(): pl.pallas_call(exchange_kernel, out_shape=jax.ShapeDtypeStruct((1, 1, NS)...  15.2 us
    pallas_call x1, Pallas kernels, image(): pl.pallas_call(image_kernel, out_shape=pltpu.VMEM((TARGETS, 2, NS), jnp.f...  3.7 us
    unnamed x4, local copies, waits for them, and re-layouts  2.79 us

profile of v3, /device:TPU:1, one launch (start us, length us, event | category | flops | bytes accessed | tf_op | source)
XLA Modules:
  0.0 56.1 jit_solution(8977969279607797093)
XLA Ops:
  0.7 0.7 %convert_reduce_fusion = f32[80]{0:T(128)S(1)} fusion(s32[80,1]{0,1:T(1,128)} %param.9, s32[80,1]{0,1:T(1,128)} %param.8), kind=kLoop, calls=%fused_computation.3 | loop fusion | flops 240 | bytes 960 | tf_op jit(solution)/shard_map/convert_element_type | solution.py:416
  1.4 1.1 %multiply_reduce_fusion = f32[2,8]{1,0:T(2,128)S(1)} fusion(bf16[2,1,1,8,8192]{4,3,2,1,0:T(8,128)(2,1)} %param.6), kind=kLoop, calls=%fused_computation | loop fusion | flops 393200 | bytes 262208 | tf_op jit(solution)/shard_map/reduce_sum | solution.py:418
  2.5 0.1 div.6
  2.6 0.1 convert_element_type.16
  2.6 0.1 reshape.20
  2.7 0.1 pad_maximum_fusion
  2.8 1.0 %copy.9 = bf16[2,8,64,128]{3,2,1,0:T(8,128)(2,1)S(1)} copy(bf16[2,8,64,128]{3,1,2,0:T(8,128)(2,1)} %bitcast.9) | data formatting | bytes 524288
  3.8 31.5 %gather_records.1 = (bf16[256,64,128]{2,1,0:T(8,128)(2,1)S(1)}, f32[128,64,128]{2,1,0:T(8,128)S(1)}, f32[128,64,128]{2,1,0:T(8,128)S(1)}, s32[8,512]{1,0:T(8,128)S(1)}, f32[16,128]{1,0:T(8,128)S(1)}) custom-call(bf16[16,64,128]{2,1,0:T(8,128)(2,1)S(1)} %bitcast.7, f32[8,128]{1,0:T(8,128)S(1)} %broadcast_in_dim.12.index, f32[128,64,128]{2,1,0:T(8,128)} %travel.1, ...), custom_call_target="tpu_custom_call" | custom-call | flops 10000000 | bytes 16000000 | tf_op jit(solution)/shard_map/gather_records/pallas_call | solution.py:249
  35.4 3.7 %image_uses.1 = f32[48,2,128]{2,1,0:T(2,128)S(1)} custom-call(s32[8,512]{1,0:T(8,128)S(1)} %get-tuple-element.10.uses, f32[16,128]{1,0:T(8,128)S(1)} %get-tuple-element.11.index, bf16[256,64,128]{2,1,0:T(8,128)(2,1)S(1)} %get-tuple-element.12.records, f32[128,64,128]{2,1,0:T(8,128)S(1)} %get-tuple-element.13.travel, f32[128,64,128]{2,1,0:T(8,128)S(1)} %get-tuple-element.14.amp), custom_call_target="tpu_custom_call" | custom-call | flops 10000000 | bytes 8000000 | tf_op jit(solution)/shard_map/image_uses/pallas_call | solution.py:320
  39.1 0.0 copy-start
  39.1 0.6 %copy-done = f32[48,2,128]{2,1,0:T(2,128)} copy-done((f32[48,2,128]{2,1,0:T(2,128)}, f32[48,2,128]{2,1,0:T(2,128)S(1)}, u32[]{:S(2)}) %copy-start) | copy-done | bytes 49176
  39.7 15.2 %exchange_sums.1 = f32[1,1,128]{2,1,0:T(1,128)} custom-call(f32[3,16,2,128]{3,2,1,0:T(2,128)} %bitcast.8), custom_call_target="tpu_custom_call" | custom-call | flops 10000 | bytes 100000 | tf_op jit(solution)/shard_map/exchange_sums/pallas_call | solution.py:394
  54.9 1.2 %copy.12 = f32[1,1,128]{2,1,0:T(1,128)} copy(f32[1,1,128]{2,1,0:T(1,128)} %exchange_sums.1) | data formatting | bytes 1024
  (4 shorter events, 0.0 us)
Async XLA Ops:
  39.1 0.6 %copy-start = (f32[48,2,128]{2,1,0:T(2,128)}, f32[48,2,128]{2,1,0:T(2,128)S(1)}, u32[]{:S(2)}) copy-start(f32[48,2,128]{2,1,0:T(2,128)S(1)} %image_uses.1) | copy-start | bytes 147460

commit v4 on v2

--- a/solution.py
+++ b/solution.py
@@ -272,7 +272,7 @@
             pltpu.SemaphoreType.DMA((COLS,)),
         ],
         compiler_params=pltpu.CompilerParams(
-            collective_id=0, has_side_effects=True, vmem_limit_bytes=32 << 20
+            collective_id=1, has_side_effects=True, vmem_limit_bytes=32 << 20
         ),
         cost_estimate=pl.CostEstimate(flops=10_000_000, bytes_accessed=16_000_000, transcendentals=0),
         name="gather_records",
@@ -405,13 +405,13 @@
             pltpu.SemaphoreType.DMA((COLS,)),
             pltpu.SemaphoreType.DMA((COLS,)),
         ],
-        compiler_params=pltpu.CompilerParams(collective_id=1, has_side_effects=True),
+        compiler_params=pltpu.CompilerParams(collective_id=2, has_side_effects=True),
         cost_estimate=pl.CostEstimate(flops=10_000, bytes_accessed=100_000, transcendentals=0),
         name="exchange_sums",
     )(sums)
 
 
-def per_device(records, beam_count, owner_list, block_list, travel_table, amp_table):
+def imaged_by_any_count(records, beam_count, owner_list, block_list, travel_table, amp_table):
     records = records.reshape(RECS, NP, NS)
     named = (owner_list * 128 + block_list)[:, 0].astype(jnp.float32)
     named = named.reshape(SHOTS, 5, BEAMS).transpose(1, 0, 2).reshape(USES)
@@ -423,6 +423,432 @@
     return exchange(sums.reshape(3, COLS, 2, NS))
 
 
+PHASES = ((0, 4, 96, 0), (4, 2, 40, 128), (6, 2, 32, 192))
+SLOTS = 256
+NBLOCKS = 128
+COPIES = 40
+
+
+def fused_kernel(
+    records, owner, block, count, travel, amp,
+    out, flag_out,
+    wide, buf0, buf1, buf2, travel_v, amp_v,
+    mine, near, mixed, lines, uses_v, uses_s,
+    con0, con1, con2, lit0, lit1, lit2,
+    flag_mine, flags, sums, parts, edge, edges,
+    local_sems, send_sems, recv_sems, near_send, near_recv, line_send, line_recv,
+    flag_send, flag_recv, part_send, part_recv, edge_send, edge_recv,
+):
+    row, col = lax.axis_index("inline"), lax.axis_index("xline")
+    z, x = col // SIDE, lax.rem(col, SIDE)
+    bufs, cons, lits = (buf0, buf1, buf2), (con0, con1, con2), (lit0, lit1, lit2)
+    near[...] = jnp.zeros_like(near)
+    edges[...] = jnp.zeros_like(edges)
+
+    barrier = pltpu.get_barrier_semaphore()
+    for other in range(1, COLS):
+        there = (row, lax.rem(col + other, COLS))
+        pl.semaphore_signal(barrier, inc=1, device_id=there, device_id_type=MESH)
+    for other in range(1, ROWS):
+        there = (lax.rem(row + other, ROWS), col)
+        pl.semaphore_signal(barrier, inc=1, device_id=there, device_id_type=MESH)
+
+    loads = [
+        pltpu.make_async_copy(travel, travel_v, local_sems.at[0]),
+        pltpu.make_async_copy(amp, amp_v, local_sems.at[1]),
+    ]
+    for copy in loads:
+        copy.start()
+
+    wide[pl.ds(0, SHOTS * NP * BEAMS), :] = records[...].astype(jnp.float32).reshape(SHOTS * NP * BEAMS, NS)
+    energies = jnp.zeros((8, NS), jnp.float32)
+    lane8 = lax.broadcasted_iota(jnp.int32, (8, NS), 1)
+    for s in range(SHOTS):
+        for p, (begin, beams, _, _) in enumerate(PHASES):
+            for b in range(beams):
+                rec = wide[pl.ds(s * NP * BEAMS + begin + b, NP, stride=BEAMS), :]
+                bufs[p][(s * COLS + col) * beams + b] = rec.astype(jnp.bfloat16)
+                energy = jnp.sum(rec * rec, keepdims=True) * (1.0 / (NP * NS))
+                energies = jnp.where(
+                    lane8 == ENERGY + s * BEAMS + begin + b, jnp.broadcast_to(energy, (8, NS)), energies
+                )
+    named = (owner[...] * 128 + block[...]).astype(jnp.float32)
+    mine[...] = jnp.where(lane8 >= COUNT, count[0, 0].astype(jnp.float32), energies)
+    mine[:, 0:USES] = jnp.broadcast_to(named, (8, USES))
+    pl.semaphore_wait(barrier, COLS + ROWS - 2)
+
+    def at(dz, dx):
+        return lax.rem(z + dz + SIDE, SIDE) * SIDE + lax.rem(x + dx + SIDE, SIDE)
+
+    started = {}
+
+    def send(key, axis, step, first, second, lo, size):
+        p, route = key[0], key[1]
+        tile = at(second, first) if route == 0 else at(first, second)
+        here = bufs[p].at[pl.ds((route * COLS + tile) * PHASES[p][1] + lo, size)]
+        along_x = (axis == 0) == (route == 0)
+        n = len(started)
+        copy = pltpu.make_async_remote_copy(
+            src_ref=here,
+            dst_ref=here,
+            send_sem=send_sems.at[n],
+            recv_sem=recv_sems.at[n],
+            device_id=(row, at(0, step) if along_x else at(step, 0)),
+            device_id_type=MESH,
+        )
+        copy.start()
+        started[key] = copy
+
+    both, ways = (0, 1), (1, -1)
+
+    def own(p):
+        beams = PHASES[p][1]
+        for route in both:
+            for step in ways:
+                send((p, route, "a", step), 0, step, 0, 0, 0, beams)
+        for route in both:
+            for way in ways:
+                send((p, route, "c", 0, way), 1, way, 0, 0, 0, beams)
+
+    def first_neighbours(p):
+        beams = PHASES[p][1]
+        half = beams // 2
+        for step in ways:
+            for route in both:
+                started[p, route, "a", step].wait_recv()
+                lo = 0 if step > 0 else half
+                send((p, route, "b", step), 0, step, -step, 0, lo, half)
+                for way in ways:
+                    send((p, route, "c", -step, way), 1, way, -step, 0, 0, beams)
+
+    def pass_on(p, which):
+        half = PHASES[p][1] // 2
+        for first in which:
+            for way in ways:
+                for route in both:
+                    started[p, route, "c", first, way].wait_recv()
+                    lo = 0 if way > 0 else half
+                    send((p, route, "d", first, way), 1, way, first, -way, lo, half)
+
+    def opposite(p):
+        for route in both:
+            for step in ways:
+                started[p, route, "b", step].wait_recv()
+            for way in ways:
+                send((p, route, "c", 2, way), 1, way, 2, 0, 0, PHASES[p][1])
+
+    def arrived(p):
+        for first in (0, -1, 1, 2):
+            for route in both:
+                for way in ways:
+                    started[p, route, "d", first, way].wait_recv()
+
+    def image_some(p, begin, end):
+        _, beams, slots, base = PHASES[p]
+        buf, con, lit = bufs[p], cons[p], lits[p]
+        held = SHOTS * COLS * beams
+
+        def step(i, carry):
+            places = [base + i * GROUP + d for d in range(GROUP)]
+            picked = [(uses_s[0, u] & (NBLOCKS - 1), uses_s[1, u] & (held - 1)) for u in places]
+            totals = [jnp.zeros((8, NS), jnp.float32) for _ in picked]
+            squares = [jnp.zeros((8, NS), jnp.float32) for _ in picked]
+            for q in range(NP // 8):
+                rows = pl.ds(8 * q, 8)
+                for d, (number, rec) in enumerate(picked):
+                    t = travel_v[number, rows, :]
+                    a = amp_v[number, rows, :]
+                    pair = buf[rec, pl.ds(16 * (q // 2), 16), :].astype(jnp.float32)
+                    r = pair[8 * (q % 2) : 8 * (q % 2) + 8]
+                    k = t.astype(jnp.int32)
+                    f = t - k.astype(jnp.float32)
+                    w0 = (1.0 - f).astype(jnp.bfloat16).astype(jnp.float32)
+                    w1 = f.astype(jnp.bfloat16).astype(jnp.float32)
+                    v0 = jnp.take_along_axis(r, k, axis=1, mode="promise_in_bounds")
+                    v1 = jnp.take_along_axis(r, k + 1, axis=1, mode="promise_in_bounds")
+                    totals[d] += a * (v0 * w0 + v1 * w1)
+                    squares[d] += a * a
+            for d in range(GROUP):
+                con[pl.ds(i * GROUP + d, 8, stride=slots), :] = totals[d]
+                lit[pl.ds(i * GROUP + d, 8, stride=slots), :] = squares[d]
+            return carry
+
+        lax.fori_loop(begin // GROUP, end // GROUP, step, 0)
+
+    def total_of(p, listed, energy):
+        _, _, slots, base = PHASES[p]
+        con = sum(cons[p][pl.ds(s * slots, slots), :] for s in range(8))
+        lit = sum(lits[p][pl.ds(s * slots, slots), :] for s in range(8))
+        target = jnp.broadcast_to(listed[2:3, base : base + slots], (NS, slots))
+        weight = jnp.broadcast_to(energy[:, base : base + slots], (NS, slots))
+        line = (lax.broadcasted_iota(jnp.int32, (NS, slots), 0) + 1).astype(jnp.float32)
+        to_con = jnp.where(target == line, 1.0, 0.0)
+        to_lit = jnp.where((target + 4.0 == line) & (target > 0.0), weight, 0.0)
+        dot = lambda m, v: jnp.dot(m, v, precision=lax.Precision.HIGHEST, preferred_element_type=jnp.float32)
+        return dot(to_con, con) + dot(to_lit, lit)
+
+    own(0)
+    own(1)
+
+    up = pltpu.make_async_remote_copy(
+        mine, near.at[0], near_send.at[0], near_recv.at[0], device_id=(row + 1, col), device_id_type=MESH
+    )
+    down = pltpu.make_async_remote_copy(
+        mine, near.at[1], near_send.at[1], near_recv.at[1], device_id=(row - 1, col), device_id_type=MESH
+    )
+    upward, downward = pl.when(row < ROWS - 1), pl.when(row > 0)
+    upward(up.start)
+    downward(down.start)
+    downward(up.wait_recv)
+    upward(down.wait_recv)
+    kind8 = lax.rem(lane8, 5 * BEAMS) // BEAMS
+    kind8 = jnp.where(lane8 < USES, kind8, 0)
+    mixed[...] = jnp.where(kind8 == 1, near[1], jnp.where(kind8 == 2, near[0], mine[...]))
+    shares = []
+    for other in range(1, COLS):
+        share = pltpu.make_async_remote_copy(
+            mixed, lines.at[other], line_send.at[other], line_recv.at[other],
+            device_id=(row, lax.rem(col + other, COLS)), device_id_type=MESH,
+        )
+        share.start()
+        shares.append(share)
+    lines[0] = mixed[...]
+
+    first_neighbours(0)
+    pass_on(0, (0,))
+    own(2)
+    first_neighbours(1)
+
+    for share in shares:
+        share.wait_recv()
+    listed, energy, over = list_uses(row, col, lines)
+    uses_v[...] = listed.astype(jnp.int32)
+    to_smem = pltpu.make_async_copy(uses_v, uses_s, local_sems.at[2])
+    to_smem.start()
+    flag_mine[...] = over
+    alarms = []
+    for other in range(1, ROWS):
+        alarm = pltpu.make_async_remote_copy(
+            flag_mine, flags.at[other], flag_send.at[other], flag_recv.at[other],
+            device_id=(lax.rem(row + other, ROWS), col), device_id_type=MESH,
+        )
+        alarm.start()
+        alarms.append(alarm)
+
+    opposite(0)
+    pass_on(0, (-1, 1))
+    pass_on(1, (0,))
+    pass_on(0, (2,))
+    opposite(1)
+    first_neighbours(2)
+    pass_on(1, (-1, 1))
+    to_smem.wait()
+    for copy in loads:
+        copy.wait()
+    arrived(0)
+    image_some(0, 0, 32)
+    pass_on(2, (0,))
+    pass_on(1, (2,))
+    opposite(2)
+    image_some(0, 32, 64)
+    pass_on(2, (-1, 1))
+    image_some(0, 64, 96)
+    pass_on(2, (2,))
+    arrived(1)
+    image_some(1, 0, 40)
+    early = total_of(0, listed, energy) + total_of(1, listed, energy)
+    raised = flag_mine[...]
+    for alarm, other in zip(alarms, range(1, ROWS)):
+        alarm.wait_recv()
+        raised = jnp.maximum(raised, flags[other])
+    flag_out[0] = jnp.max(raised).astype(jnp.int32)
+    arrived(2)
+    image_some(2, 0, 32)
+    sums[...] = (early + total_of(2, listed, energy)).reshape(COLS, 8, NS)
+
+    pieces = []
+    for other in range(1, COLS):
+        there = lax.rem(col + other, COLS)
+        piece = pltpu.make_async_remote_copy(
+            sums.at[there], parts.at[other], part_send.at[other], part_recv.at[other],
+            device_id=(row, there), device_id_type=MESH,
+        )
+        piece.start()
+        pieces.append(piece)
+    whole = sums[col]
+    for piece, other in zip(pieces, range(1, COLS)):
+        piece.wait_recv()
+        whole += parts[other]
+    edge[...] = whole
+    to_next = pltpu.make_async_remote_copy(
+        edge, edges.at[0], edge_send.at[0], edge_recv.at[0], device_id=(row + 1, col), device_id_type=MESH
+    )
+    to_prev = pltpu.make_async_remote_copy(
+        edge, edges.at[1], edge_send.at[1], edge_recv.at[1], device_id=(row - 1, col), device_id_type=MESH
+    )
+    upward(to_next.start)
+    downward(to_prev.start)
+    for copy in started.values():
+        copy.wait_send()
+    for copy in shares + alarms + pieces:
+        copy.wait_send()
+    upward(up.wait_send)
+    downward(down.wait_send)
+    downward(to_next.wait_recv)
+    upward(to_prev.wait_recv)
+    contrib = whole[1:2] + edges[0][2:3] + edges[1][0:1]
+    lighting = whole[5:6] + edges[0][6:7] + edges[1][4:5]
+    out[0] = contrib / jnp.sqrt(1.0 + lighting)
+    upward(to_next.wait_send)
+    downward(to_prev.wait_send)
+
+
+def list_uses(row, col, lines):
+    table = jnp.concatenate([lines[lax.rem(col - tile + COLS, COLS)][0:1, :] for tile in range(COLS)], axis=0)
+    shape = (COLS, NS)
+    lane = lax.broadcasted_iota(jnp.int32, shape, 1)
+    tile = lax.broadcasted_iota(jnp.int32, shape, 0)
+    shot, kind, beam = lane // (5 * BEAMS), lax.rem(lane, 5 * BEAMS) // BEAMS, lax.rem(lane, BEAMS)
+    names = table.astype(jnp.int32)
+
+    def of_source(own):
+        before, after = pltpu.roll(own, 1, 0), pltpu.roll(own, COLS - 1, 0)
+        return jnp.where(kind == 3, before, jnp.where(kind == 4, after, own))
+
+    last, first = (row == ROWS - 1).astype(jnp.int32), (row == 0).astype(jnp.int32)
+    missing = (
+        ((kind == 1) & (last == 1))
+        | ((kind == 2) & (first == 1))
+        | ((kind == 3) & (tile == 0))
+        | ((kind == 4) & (tile == COLS - 1))
+    )
+    counts = of_source(jnp.broadcast_to(names[:, COUNT : COUNT + 1], shape))
+    energy = of_source(
+        jnp.take_along_axis(
+            table, jnp.where(lane < USES, ENERGY + shot * BEAMS + beam, lane), axis=1, mode="promise_in_bounds"
+        )
+    )
+    live = (lane < USES) & (beam < counts) & jnp.logical_not(missing)
+    owners = jnp.where(live, names // 128, -1)
+
+    per_owner = jnp.concatenate(
+        [jnp.sum((owners == o).astype(jnp.float32), axis=0, keepdims=True) for o in range(COLS)], axis=0
+    )
+    source_beam = lax.rem(lax.broadcasted_iota(jnp.int32, (NS, NS), 0), BEAMS)
+    column = lax.broadcasted_iota(jnp.int32, (NS, NS), 1)
+    pick = jnp.zeros((NS, NS), jnp.bool_)
+    limit = jnp.full(shape, float(LIST))
+    for p, (begin, beams, slots, _) in enumerate(PHASES):
+        pick = pick | ((column == p) & (source_beam >= begin) & (source_beam < begin + beams))
+        limit = jnp.where(lane == p, float(slots), limit)
+    held = jnp.dot(per_owner, pick.astype(jnp.float32), preferred_element_type=jnp.float32)
+    over = jnp.max((held > limit).astype(jnp.float32), keepdims=True)
+
+    earlier = lax.broadcasted_iota(jnp.int32, (NS, NS), 0) <= column
+    above = lax.broadcasted_iota(jnp.int32, (COLS, COLS), 1) < lax.broadcasted_iota(jnp.int32, (COLS, COLS), 0)
+    source = tile + (kind == 4).astype(jnp.int32) - (kind == 3).astype(jnp.int32)
+    shift = 1 + (kind == 1).astype(jnp.int32) - (kind == 2).astype(jnp.int32)
+    place = jnp.full(shape, -1.0)
+    record = jnp.zeros(shape, jnp.int32)
+    for begin, beams, slots, base in PHASES:
+        marks = (owners == col) & (beam >= begin) & (beam < begin + beams)
+        ones = marks.astype(jnp.float32)
+        within = jnp.dot(ones, earlier.astype(jnp.float32), preferred_element_type=jnp.float32)
+        totals = jnp.broadcast_to(jnp.sum(ones, axis=1, keepdims=True), shape)
+        ahead = jnp.dot(above.astype(jnp.float32), totals, preferred_element_type=jnp.float32)
+        rank = within + ahead - 1.0
+        place = jnp.where(marks & (rank < float(slots)), rank + float(base), place)
+        record = jnp.where(marks, (shot * COLS + source) * beams + beam - begin, record)
+    high = energy.astype(jnp.bfloat16).astype(jnp.float32)
+    middle = (energy - high).astype(jnp.bfloat16).astype(jnp.float32)
+    low = energy - high - middle
+    fields = (
+        lax.rem(names, 128).astype(jnp.float32),
+        record.astype(jnp.float32),
+        (tile * 8 + shift + 1).astype(jnp.float32),
+        high,
+        middle,
+        low,
+    )
+    upright = jnp.transpose(place)
+    slot = lax.broadcasted_iota(jnp.int32, (NS, SLOTS), 1).astype(jnp.float32)
+    line = lax.broadcasted_iota(jnp.int32, (8, NS), 0)
+    listed = jnp.zeros((8, SLOTS), jnp.float32)
+    for t in range(COLS):
+        here = (jnp.broadcast_to(upright[:, t : t + 1], (NS, SLOTS)) == slot).astype(jnp.bfloat16)
+        rows = jnp.zeros((8, NS), jnp.float32)
+        for f, field in enumerate(fields):
+            rows = jnp.where(line == f, jnp.broadcast_to(field[t : t + 1, :], (8, NS)), rows)
+        listed += jnp.dot(rows.astype(jnp.bfloat16), here, preferred_element_type=jnp.float32)
+    return listed, listed[3:4] + listed[4:5] + listed[5:6], jnp.broadcast_to(over, (8, NS))
+
+
+def fused(records, owner, block, count, travel, amp):
+    vmem = pl.BlockSpec(memory_space=pltpu.VMEM)
+    smem = pl.BlockSpec(memory_space=pltpu.SMEM)
+    hbm = pl.BlockSpec(memory_space=pl.ANY)
+    dma = pltpu.SemaphoreType.DMA
+    f32 = jnp.float32
+    many = COPIES * len(PHASES)
+    return pl.pallas_call(
+        fused_kernel,
+        out_shape=(jax.ShapeDtypeStruct((1, 1, NS), f32), jax.ShapeDtypeStruct((1,), jnp.int32)),
+        in_specs=[vmem, vmem, vmem, smem, hbm, hbm],
+        out_specs=(vmem, smem),
+        scratch_shapes=[
+            pltpu.VMEM(((SHOTS * NP + 1) * BEAMS, NS), f32),
+            *[pltpu.VMEM((SHOTS * COLS * beams, NP, NS), jnp.bfloat16) for _, beams, _, _ in PHASES],
+            pltpu.VMEM(travel.shape, f32),
+            pltpu.VMEM(amp.shape, f32),
+            pltpu.VMEM((8, NS), f32),
+            pltpu.VMEM((2, 8, NS), f32),
+            pltpu.VMEM((8, NS), f32),
+            pltpu.VMEM((COLS, 8, NS), f32),
+            pltpu.VMEM((8, SLOTS), jnp.int32),
+            pltpu.SMEM((8, SLOTS), jnp.int32),
+            *[pltpu.VMEM((9 * slots, NS), f32) for _, _, slots, _ in PHASES],
+            *[pltpu.VMEM((9 * slots, NS), f32) for _, _, slots, _ in PHASES],
+            pltpu.VMEM((8, NS), f32),
+            pltpu.VMEM((ROWS, 8, NS), f32),
+            pltpu.VMEM((COLS, 8, NS), f32),
+            pltpu.VMEM((COLS, 8, NS), f32),
+            pltpu.VMEM((8, NS), f32),
+            pltpu.VMEM((2, 8, NS), f32),
+            dma((3,)),
+            dma((many,)),
+            dma((many,)),
+            dma((2,)),
+            dma((2,)),
+            dma((COLS,)),
+            dma((COLS,)),
+            dma((ROWS,)),
+            dma((ROWS,)),
+            dma((COLS,)),
+            dma((COLS,)),
+            dma((2,)),
+            dma((2,)),
+        ],
+        compiler_params=pltpu.CompilerParams(
+            collective_id=0, has_side_effects=True, vmem_limit_bytes=40 << 20
+        ),
+        cost_estimate=pl.CostEstimate(flops=10_000_000, bytes_accessed=16_000_000, transcendentals=0),
+        name="migrate",
+    )(records, owner, block, count, travel, amp)
+
+
+def per_device(records, beam_count, owner_list, block_list, travel_table, amp_table):
+    travel_table = pltpu.with_memory_space_constraint(travel_table, pltpu.HBM)
+    amp_table = pltpu.with_memory_space_constraint(amp_table, pltpu.HBM)
+    by_slowness = records.reshape(SHOTS, BEAMS, NP, NS).transpose(0, 2, 1, 3)
+    owner, block = owner_list.reshape(1, USES), block_list.reshape(1, USES)
+    quick, flag = fused(by_slowness, owner, block, beam_count, travel_table, amp_table)
+    return lax.cond(
+        flag[0] > 0,
+        lambda: imaged_by_any_count(records, beam_count, owner_list, block_list, travel_table, amp_table),
+        lambda: quick,
+    )
+
+
 def solution(mesh):
     placed = (
         P(None, "inline", "xline", None, None),

time: 62.6 us -> 52.9 us (0.85)
  local copies, waits for them, and re-layouts: 7.43 us -> 0.53 us
  other arithmetic: 1.89 us -> 0 us
  Pallas kernels: 52.3 us -> 50.9 us
  between operations: 0.71 us -> 1.35 us
    unnamed x8 -> x7, local copies, waits for them, and re-layouts: 7.16 us -> 0.53 us
    pallas_call x3 -> x1, Pallas kernels: 52.3 us -> 50.9 us  [fused(): pl.pallas_call(fused_kernel, out_shape=(jax.ShapeDtypeStruct((1, 1, NS),...]
    reduce_sum x1 -> x0, other arithmetic: 1.11 us -> none  [per_device(): energy = jnp.mean(jnp.square(records.astype(jnp.float32)), axis=(1, 2))]
    convert_element_type x1 -> x0, other arithmetic: 0.69 us -> none  [per_device(): named = (owner_list * 128 + block_list)[:, 0].astype(jnp.float32)]
where the time goes in v4:
time: 52.9 us; the launch traced here: 52.7 us
  Pallas kernels  50.9 us (96%)
  between operations  1.35 us (3%)
  local copies, waits for them, and re-layouts  0.53 us (1%)
    pallas_call x1, Pallas kernels, fused(): pl.pallas_call(fused_kernel, out_shape=(jax.ShapeDtypeStruct((1, 1, NS),...  50.9 us

profile of v4, /device:TPU:1, one launch (start us, length us, event | category | flops | bytes accessed | tf_op | source)
XLA Modules:
  0.0 52.7 jit_solution(7404240007951769105)
XLA Ops:
  0.7 0.0 copy-start.1
  0.7 0.0 copy-start.2
  0.7 0.0 copy-start.3
  0.7 50.9 %migrate.1 = (f32[1,1,128]{2,1,0:T(1,128)S(1)}, s32[1]{0:T(128)}) custom-call(bf16[2,64,8,128]{3,2,1,0:T(8,128)(2,1)} %bitcast.18, s32[1,80]{1,0:T(1,128)} %bitcast.21, s32[1,80]{1,0:T(1,128)} %bitcast.22, s32[1,1]{1,0:T(1,128)S(6)} %copy.17.count, f32[128,64,128]{2,1,0:T(8,128)} %travel.1, f32[128,64,128]{2,1,0:T(8,128)} %amp.1), custom_call_target="tpu_custom_call" | custom-call | flops 10000000 | bytes 16000000 | tf_op jit(solution)/shard_map/migrate/pallas_call | solution.py:793
  52.2 0.0 copy-done.1
  52.2 0.0 copy-done.2
  52.2 0.0 copy-done.3
  52.2 0.5 copy.18
  (1 shorter events, 0.0 us)
Async XLA Ops:
  0.7 51.5 %copy-start.1 = (bf16[2,1,1,8,8192]{4,3,2,1,0:T(8,128)(2,1)S(1)}, bf16[2,1,1,8,8192]{4,3,2,1,0:T(8,128)(2,1)}, u32[]{:S(2)}) copy-start(bf16[2,1,1,8,8192]{4,3,2,1,0:T(8,128)(2,1)} %param.8) | copy-start | bytes 786436
  0.7 51.5 %copy-start.2 = (s32[80,1]{0,1:T(1,128)S(1)}, s32[80,1]{0,1:T(1,128)}, u32[]{:S(2)}) copy-start(s32[80,1]{0,1:T(1,128)} %param.10) | copy-start | bytes 964
  0.7 51.5 %copy-start.3 = (s32[80,1]{0,1:T(1,128)S(1)}, s32[80,1]{0,1:T(1,128)}, u32[]{:S(2)}) copy-start(s32[80,1]{0,1:T(1,128)} %param.11) | copy-start | bytes 964

commit v5 on v4

--- a/solution.py
+++ b/solution.py
@@ -423,25 +423,37 @@
     return exchange(sums.reshape(3, COLS, 2, NS))
 
 
-PHASES = ((0, 4, 96, 0), (4, 2, 40, 128), (6, 2, 32, 192))
+CLASSES = (
+    (((0, 0), (1, 0), (-1, 0), (2, 0)), 56, 0, 64),
+    (((0, 1), (0, -1), (1, 1), (1, -1), (-1, 1), (-1, -1)), 80, 64, 128),
+    (((2, 1), (2, -1), (0, 2)), 40, 144, 64),
+    (((1, 2), (-1, 2)), 32, 184, 32),
+    (((2, 2),), 24, 216, 16),
+)
+WHERE = {tile: (c, n) for c, (tiles, _, _, _) in enumerate(CLASSES) for n, tile in enumerate(tiles)}
 SLOTS = 256
 NBLOCKS = 128
 COPIES = 40
 
 
+def wrap(steps):
+    return (steps + 1) % SIDE - 1
+
+
 def fused_kernel(
     records, owner, block, count, travel, amp,
     out, flag_out,
-    wide, buf0, buf1, buf2, travel_v, amp_v,
+    wide, buf0, buf1, buf2, buf3, buf4, travel_v, amp_v,
     mine, near, mixed, lines, uses_v, uses_s,
-    con0, con1, con2, lit0, lit1, lit2,
+    con0, con1, con2, con3, con4, lit0, lit1, lit2, lit3, lit4,
     flag_mine, flags, sums, parts, edge, edges,
     local_sems, send_sems, recv_sems, near_send, near_recv, line_send, line_recv,
     flag_send, flag_recv, part_send, part_recv, edge_send, edge_recv,
 ):
     row, col = lax.axis_index("inline"), lax.axis_index("xline")
     z, x = col // SIDE, lax.rem(col, SIDE)
-    bufs, cons, lits = (buf0, buf1, buf2), (con0, con1, con2), (lit0, lit1, lit2)
+    bufs = (buf0, buf1, buf2, buf3, buf4)
+    cons, lits = (con0, con1, con2, con3, con4), (lit0, lit1, lit2, lit3, lit4)
     near[...] = jnp.zeros_like(near)
     edges[...] = jnp.zeros_like(edges)
 
@@ -464,14 +476,11 @@
     energies = jnp.zeros((8, NS), jnp.float32)
     lane8 = lax.broadcasted_iota(jnp.int32, (8, NS), 1)
     for s in range(SHOTS):
-        for p, (begin, beams, _, _) in enumerate(PHASES):
-            for b in range(beams):
-                rec = wide[pl.ds(s * NP * BEAMS + begin + b, NP, stride=BEAMS), :]
-                bufs[p][(s * COLS + col) * beams + b] = rec.astype(jnp.bfloat16)
-                energy = jnp.sum(rec * rec, keepdims=True) * (1.0 / (NP * NS))
-                energies = jnp.where(
-                    lane8 == ENERGY + s * BEAMS + begin + b, jnp.broadcast_to(energy, (8, NS)), energies
-                )
+        for b in range(BEAMS):
+            rec = wide[pl.ds(s * NP * BEAMS + b, NP, stride=BEAMS), :]
+            bufs[0][row_of(s, 0, 0) + b] = rec.astype(jnp.bfloat16)
+            energy = jnp.sum(rec * rec, keepdims=True) * (1.0 / (NP * NS))
+            energies = jnp.where(lane8 == ENERGY + s * BEAMS + b, jnp.broadcast_to(energy, (8, NS)), energies)
     named = (owner[...] * 128 + block[...]).astype(jnp.float32)
     mine[...] = jnp.where(lane8 >= COUNT, count[0, 0].astype(jnp.float32), energies)
     mine[:, 0:USES] = jnp.broadcast_to(named, (8, USES))
@@ -482,71 +491,45 @@
 
     started = {}
 
-    def send(key, axis, step, first, second, lo, size):
-        p, route = key[0], key[1]
-        tile = at(second, first) if route == 0 else at(first, second)
-        here = bufs[p].at[pl.ds((route * COLS + tile) * PHASES[p][1] + lo, size)]
+    def send(kind, route, axis, step, first, second, lo, size):
+        seen = (wrap(first - step), second) if axis == 0 else (first, wrap(second - step))
+        here, there = WHERE[first, second][0], WHERE[seen][0]
         along_x = (axis == 0) == (route == 0)
         n = len(started)
         copy = pltpu.make_async_remote_copy(
-            src_ref=here,
-            dst_ref=here,
+            src_ref=bufs[here].at[pl.ds(row_of(route, first, second) + lo, size)],
+            dst_ref=bufs[there].at[pl.ds(row_of(route, *seen) + lo, size)],
             send_sem=send_sems.at[n],
             recv_sem=recv_sems.at[n],
             device_id=(row, at(0, step) if along_x else at(step, 0)),
             device_id_type=MESH,
         )
         copy.start()
+        key = (kind, route, step) if axis == 0 else (kind, route, first, step)
         started[key] = copy
 
     both, ways = (0, 1), (1, -1)
-
-    def own(p):
-        beams = PHASES[p][1]
-        for route in both:
-            for step in ways:
-                send((p, route, "a", step), 0, step, 0, 0, 0, beams)
+    half = BEAMS // 2
+
+    def along_second(first):
+        for way in ways:
+            for route in both:
+                send("c", route, 1, way, first, 0, 0, BEAMS)
+
+    def pass_on(first):
+        for way in ways:
+            for route in both:
+                started["c", route, first, way].wait_recv()
+                send("d", route, 1, way, first, -way, 0 if way > 0 else half, half)
+
+    def arrived(first):
         for route in both:
             for way in ways:
-                send((p, route, "c", 0, way), 1, way, 0, 0, 0, beams)
-
-    def first_neighbours(p):
-        beams = PHASES[p][1]
-        half = beams // 2
-        for step in ways:
-            for route in both:
-                started[p, route, "a", step].wait_recv()
-                lo = 0 if step > 0 else half
-                send((p, route, "b", step), 0, step, -step, 0, lo, half)
-                for way in ways:
-                    send((p, route, "c", -step, way), 1, way, -step, 0, 0, beams)
-
-    def pass_on(p, which):
-        half = PHASES[p][1] // 2
-        for first in which:
-            for way in ways:
-                for route in both:
-                    started[p, route, "c", first, way].wait_recv()
-                    lo = 0 if way > 0 else half
-                    send((p, route, "d", first, way), 1, way, first, -way, lo, half)
-
-    def opposite(p):
-        for route in both:
-            for step in ways:
-                started[p, route, "b", step].wait_recv()
-            for way in ways:
-                send((p, route, "c", 2, way), 1, way, 2, 0, 0, PHASES[p][1])
-
-    def arrived(p):
-        for first in (0, -1, 1, 2):
-            for route in both:
-                for way in ways:
-                    started[p, route, "d", first, way].wait_recv()
+                started["d", route, first, way].wait_recv()
 
     def image_some(p, begin, end):
-        _, beams, slots, base = PHASES[p]
+        _, slots, base, held = CLASSES[p]
         buf, con, lit = bufs[p], cons[p], lits[p]
-        held = SHOTS * COLS * beams
 
         def step(i, carry):
             places = [base + i * GROUP + d for d in range(GROUP)]
@@ -576,7 +559,7 @@
         lax.fori_loop(begin // GROUP, end // GROUP, step, 0)
 
     def total_of(p, listed, energy):
-        _, _, slots, base = PHASES[p]
+        _, slots, base, _ = CLASSES[p]
         con = sum(cons[p][pl.ds(s * slots, slots), :] for s in range(8))
         lit = sum(lits[p][pl.ds(s * slots, slots), :] for s in range(8))
         target = jnp.broadcast_to(listed[2:3, base : base + slots], (NS, slots))
@@ -587,8 +570,10 @@
         dot = lambda m, v: jnp.dot(m, v, precision=lax.Precision.HIGHEST, preferred_element_type=jnp.float32)
         return dot(to_con, con) + dot(to_lit, lit)
 
-    own(0)
-    own(1)
+    for step in ways:
+        for route in both:
+            send("a", route, 0, step, 0, 0, 0, BEAMS)
+    along_second(0)
 
     up = pltpu.make_async_remote_copy(
         mine, near.at[0], near_send.at[0], near_recv.at[0], device_id=(row + 1, col), device_id_type=MESH
@@ -614,10 +599,11 @@
         shares.append(share)
     lines[0] = mixed[...]
 
-    first_neighbours(0)
-    pass_on(0, (0,))
-    own(2)
-    first_neighbours(1)
+    for step in ways:
+        for route in both:
+            started["a", route, step].wait_recv()
+            send("b", route, 0, step, -step, 0, 0 if step > 0 else half, half)
+        along_second(-step)
 
     for share in shares:
         share.wait_recv()
@@ -635,36 +621,34 @@
         alarm.start()
         alarms.append(alarm)
 
-    opposite(0)
-    pass_on(0, (-1, 1))
-    pass_on(1, (0,))
-    pass_on(0, (2,))
-    opposite(1)
-    first_neighbours(2)
-    pass_on(1, (-1, 1))
+    pass_on(0)
+    for route in both:
+        for step in ways:
+            started["b", route, step].wait_recv()
+    along_second(2)
     to_smem.wait()
     for copy in loads:
         copy.wait()
+    image_some(0, 0, 56)
+    pass_on(1)
+    pass_on(-1)
+    image_some(1, 0, 80)
+    pass_on(2)
     arrived(0)
-    image_some(0, 0, 32)
-    pass_on(2, (0,))
-    pass_on(1, (2,))
-    opposite(2)
-    image_some(0, 32, 64)
-    pass_on(2, (-1, 1))
-    image_some(0, 64, 96)
-    pass_on(2, (2,))
-    arrived(1)
-    image_some(1, 0, 40)
-    early = total_of(0, listed, energy) + total_of(1, listed, energy)
+    image_some(2, 0, 40)
+    early = total_of(0, listed, energy) + total_of(1, listed, energy) + total_of(2, listed, energy)
     raised = flag_mine[...]
     for alarm, other in zip(alarms, range(1, ROWS)):
         alarm.wait_recv()
         raised = jnp.maximum(raised, flags[other])
     flag_out[0] = jnp.max(raised).astype(jnp.int32)
+    arrived(1)
+    arrived(-1)
+    image_some(3, 0, 32)
+    early += total_of(3, listed, energy)
     arrived(2)
-    image_some(2, 0, 32)
-    sums[...] = (early + total_of(2, listed, energy)).reshape(COLS, 8, NS)
+    image_some(4, 0, 24)
+    sums[...] = (early + total_of(4, listed, energy)).reshape(COLS, 8, NS)
 
     pieces = []
     for other in range(1, COLS):
@@ -703,6 +687,11 @@
     downward(to_prev.wait_send)
 
 
+def row_of(route, first, second):
+    c, n = WHERE[first, second]
+    return (route * len(CLASSES[c][0]) + n) * BEAMS
+
+
 def list_uses(row, col, lines):
     table = jnp.concatenate([lines[lax.rem(col - tile + COLS, COLS)][0:1, :] for tile in range(COLS)], axis=0)
     shape = (COLS, NS)
@@ -729,36 +718,41 @@
         )
     )
     live = (lane < USES) & (beam < counts) & jnp.logical_not(missing)
-    owners = jnp.where(live, names // 128, -1)
-
-    per_owner = jnp.concatenate(
-        [jnp.sum((owners == o).astype(jnp.float32), axis=0, keepdims=True) for o in range(COLS)], axis=0
-    )
-    source_beam = lax.rem(lax.broadcasted_iota(jnp.int32, (NS, NS), 0), BEAMS)
+    owners = names // 128
+
+    source = tile + (kind == 4).astype(jnp.int32) - (kind == 3).astype(jnp.int32)
+    along_z = (source // SIDE - owners // SIDE) & (SIDE - 1)
+    along_x = (source - owners) & (SIDE - 1)
+    code = jnp.where(shot == 0, along_x * SIDE + along_z, along_z * SIDE + along_x)
+    group, record = jnp.zeros(shape, jnp.int32), jnp.zeros(shape, jnp.int32)
+    for (first_step, second_step), (c, _) in WHERE.items():
+        same = code == first_step % SIDE * SIDE + second_step % SIDE
+        group = jnp.where(same, c, group)
+        begin = [row_of(route, first_step, second_step) for route in (0, 1)]
+        record = jnp.where(same, jnp.where(shot == 0, begin[0], begin[1]) + beam, record)
+
     column = lax.broadcasted_iota(jnp.int32, (NS, NS), 1)
-    pick = jnp.zeros((NS, NS), jnp.bool_)
-    limit = jnp.full(shape, float(LIST))
-    for p, (begin, beams, slots, _) in enumerate(PHASES):
-        pick = pick | ((column == p) & (source_beam >= begin) & (source_beam < begin + beams))
-        limit = jnp.where(lane == p, float(slots), limit)
-    held = jnp.dot(per_owner, pick.astype(jnp.float32), preferred_element_type=jnp.float32)
-    over = jnp.max((held > limit).astype(jnp.float32), keepdims=True)
+    owned = jnp.where(live, owners * 8 + group, -1)
+    over = jnp.zeros((1, 1), jnp.float32)
+    for c, (_, slots, _, _) in enumerate(CLASSES):
+        per_owner = jnp.concatenate(
+            [jnp.sum((owned == o * 8 + c).astype(jnp.float32), axis=0, keepdims=True) for o in range(COLS)], axis=0
+        )
+        held = jnp.sum(per_owner, axis=1, keepdims=True)
+        over = jnp.maximum(over, jnp.max((held > float(slots)).astype(jnp.float32), keepdims=True))
 
     earlier = lax.broadcasted_iota(jnp.int32, (NS, NS), 0) <= column
     above = lax.broadcasted_iota(jnp.int32, (COLS, COLS), 1) < lax.broadcasted_iota(jnp.int32, (COLS, COLS), 0)
-    source = tile + (kind == 4).astype(jnp.int32) - (kind == 3).astype(jnp.int32)
     shift = 1 + (kind == 1).astype(jnp.int32) - (kind == 2).astype(jnp.int32)
     place = jnp.full(shape, -1.0)
-    record = jnp.zeros(shape, jnp.int32)
-    for begin, beams, slots, base in PHASES:
-        marks = (owners == col) & (beam >= begin) & (beam < begin + beams)
+    for c, (_, slots, base, _) in enumerate(CLASSES):
+        marks = live & (owners == col) & (group == c)
         ones = marks.astype(jnp.float32)
         within = jnp.dot(ones, earlier.astype(jnp.float32), preferred_element_type=jnp.float32)
         totals = jnp.broadcast_to(jnp.sum(ones, axis=1, keepdims=True), shape)
         ahead = jnp.dot(above.astype(jnp.float32), totals, preferred_element_type=jnp.float32)
         rank = within + ahead - 1.0
         place = jnp.where(marks & (rank < float(slots)), rank + float(base), place)
-        record = jnp.where(marks, (shot * COLS + source) * beams + beam - begin, record)
     high = energy.astype(jnp.bfloat16).astype(jnp.float32)
     middle = (energy - high).astype(jnp.bfloat16).astype(jnp.float32)
     low = energy - high - middle
@@ -789,7 +783,6 @@
     hbm = pl.BlockSpec(memory_space=pl.ANY)
     dma = pltpu.SemaphoreType.DMA
     f32 = jnp.float32
-    many = COPIES * len(PHASES)
     return pl.pallas_call(
         fused_kernel,
         out_shape=(jax.ShapeDtypeStruct((1, 1, NS), f32), jax.ShapeDtypeStruct((1,), jnp.int32)),
@@ -797,7 +790,7 @@
         out_specs=(vmem, smem),
         scratch_shapes=[
             pltpu.VMEM(((SHOTS * NP + 1) * BEAMS, NS), f32),
-            *[pltpu.VMEM((SHOTS * COLS * beams, NP, NS), jnp.bfloat16) for _, beams, _, _ in PHASES],
+            *[pltpu.VMEM((held, NP, NS), jnp.bfloat16) for _, _, _, held in CLASSES],
             pltpu.VMEM(travel.shape, f32),
             pltpu.VMEM(amp.shape, f32),
             pltpu.VMEM((8, NS), f32),
@@ -806,8 +799,8 @@
             pltpu.VMEM((COLS, 8, NS), f32),
             pltpu.VMEM((8, SLOTS), jnp.int32),
             pltpu.SMEM((8, SLOTS), jnp.int32),
-            *[pltpu.VMEM((9 * slots, NS), f32) for _, _, slots, _ in PHASES],
-            *[pltpu.VMEM((9 * slots, NS), f32) for _, _, slots, _ in PHASES],
+            *[pltpu.VMEM((9 * slots, NS), f32) for _, slots, _, _ in CLASSES],
+            *[pltpu.VMEM((9 * slots, NS), f32) for _, slots, _, _ in CLASSES],
             pltpu.VMEM((8, NS), f32),
             pltpu.VMEM((ROWS, 8, NS), f32),
             pltpu.VMEM((COLS, 8, NS), f32),
@@ -815,8 +808,8 @@
             pltpu.VMEM((8, NS), f32),
             pltpu.VMEM((2, 8, NS), f32),
             dma((3,)),
-            dma((many,)),
-            dma((many,)),
+            dma((COPIES,)),
+            dma((COPIES,)),
             dma((2,)),
             dma((2,)),
             dma((COLS,)),

time: 52.9 us -> 47.7 us (0.902)
  Pallas kernels: 50.9 us -> 45.6 us
    pallas_call x1, Pallas kernels: 50.9 us -> 45.6 us  [fused(): pl.pallas_call(fused_kernel, out_shape=(jax.ShapeDtypeStruct((1, 1, NS),...]
where the time goes in v5:
time: 47.7 us; the launch traced here: 47.5 us
  Pallas kernels  45.6 us (96%)
  between operations  1.35 us (3%)
  local copies, waits for them, and re-layouts  0.53 us (1%)
    pallas_call x1, Pallas kernels, fused(): pl.pallas_call(fused_kernel, out_shape=(jax.ShapeDtypeStruct((1, 1, NS),...  45.6 us

profile of v5, /device:TPU:1, one launch (start us, length us, event | category | flops | bytes accessed | tf_op | source)
XLA Modules:
  0.0 47.5 jit_solution(8205385697852471875)
XLA Ops:
  0.7 0.0 copy-start.1
  0.7 0.0 copy-start.2
  0.7 0.0 copy-start.3
  0.7 45.6 %migrate.1 = (f32[1,1,128]{2,1,0:T(1,128)S(1)}, s32[1]{0:T(128)}) custom-call(bf16[2,64,8,128]{3,2,1,0:T(8,128)(2,1)} %bitcast.18, s32[1,80]{1,0:T(1,128)} %bitcast.21, s32[1,80]{1,0:T(1,128)} %bitcast.22, s32[1,1]{1,0:T(1,128)S(6)} %copy.17.count, f32[128,64,128]{2,1,0:T(8,128)} %travel.1, f32[128,64,128]{2,1,0:T(8,128)} %amp.1), custom_call_target="tpu_custom_call" | custom-call | flops 10000000 | bytes 16000000 | tf_op jit(solution)/shard_map/migrate/pallas_call | solution.py:786
  47.0 0.0 copy-done.1
  47.0 0.0 copy-done.2
  47.0 0.0 copy-done.3
  47.0 0.5 %copy.18 = f32[1,1,128]{2,1,0:T(1,128)} copy(f32[1,1,128]{2,1,0:T(1,128)S(1)} %get-tuple-element.36) | data formatting | bytes 1024
  (1 shorter events, 0.0 us)
Async XLA Ops:
  0.7 46.3 %copy-start.1 = (bf16[2,1,1,8,8192]{4,3,2,1,0:T(8,128)(2,1)S(1)}, bf16[2,1,1,8,8192]{4,3,2,1,0:T(8,128)(2,1)}, u32[]{:S(2)}) copy-start(bf16[2,1,1,8,8192]{4,3,2,1,0:T(8,128)(2,1)} %param.8) | copy-start | bytes 786436
  0.7 46.3 %copy-start.2 = (s32[80,1]{0,1:T(1,128)S(1)}, s32[80,1]{0,1:T(1,128)}, u32[]{:S(2)}) copy-start(s32[80,1]{0,1:T(1,128)} %param.10) | copy-start | bytes 964
  0.7 46.3 %copy-start.3 = (s32[80,1]{0,1:T(1,128)S(1)}, s32[80,1]{0,1:T(1,128)}, u32[]{:S(2)}) copy-start(s32[80,1]{0,1:T(1,128)} %param.11) | copy-start | bytes 964

commit v6 on v5

--- a/solution.py
+++ b/solution.py
@@ -446,7 +446,7 @@
     wide, buf0, buf1, buf2, buf3, buf4, travel_v, amp_v,
     mine, near, mixed, lines, uses_v, uses_s,
     con0, con1, con2, con3, con4, lit0, lit1, lit2, lit3, lit4,
-    flag_mine, flags, sums, parts, edge, edges,
+    flag_mine, flags, sums, parts, edge, edges, records_v, owner_v, block_v, met,
     local_sems, send_sems, recv_sems, near_send, near_recv, line_send, line_recv,
     flag_send, flag_recv, part_send, part_recv, edge_send, edge_recv,
 ):
@@ -457,14 +457,21 @@
     near[...] = jnp.zeros_like(near)
     edges[...] = jnp.zeros_like(edges)
 
+    def at(dz, dx):
+        return lax.rem(z + dz + SIDE, SIDE) * SIDE + lax.rem(x + dx + SIDE, SIDE)
+
+    beside = [(row, at(dz, dx)) for dz, dx in ((0, 1), (0, -1), (1, 0), (-1, 0))]
+    beside += [(lax.rem(row + 1, ROWS), col), (lax.rem(row + ROWS - 1, ROWS), col)]
     barrier = pltpu.get_barrier_semaphore()
-    for other in range(1, COLS):
-        there = (row, lax.rem(col + other, COLS))
+    for there in beside:
         pl.semaphore_signal(barrier, inc=1, device_id=there, device_id_type=MESH)
-    for other in range(1, ROWS):
-        there = (lax.rem(row + other, ROWS), col)
-        pl.semaphore_signal(barrier, inc=1, device_id=there, device_id_type=MESH)
-
+    inputs = [
+        pltpu.make_async_copy(records, records_v, local_sems.at[3]),
+        pltpu.make_async_copy(owner, owner_v, local_sems.at[4]),
+        pltpu.make_async_copy(block, block_v, local_sems.at[5]),
+    ]
+    for copy in inputs:
+        copy.start()
     loads = [
         pltpu.make_async_copy(travel, travel_v, local_sems.at[0]),
         pltpu.make_async_copy(amp, amp_v, local_sems.at[1]),
@@ -472,7 +479,10 @@
     for copy in loads:
         copy.start()
 
-    wide[pl.ds(0, SHOTS * NP * BEAMS), :] = records[...].astype(jnp.float32).reshape(SHOTS * NP * BEAMS, NS)
+    for copy in inputs:
+        copy.wait()
+
+    wide[pl.ds(0, SHOTS * NP * BEAMS), :] = records_v[...].astype(jnp.float32).reshape(SHOTS * NP * BEAMS, NS)
     energies = jnp.zeros((8, NS), jnp.float32)
     lane8 = lax.broadcasted_iota(jnp.int32, (8, NS), 1)
     for s in range(SHOTS):
@@ -481,13 +491,10 @@
             bufs[0][row_of(s, 0, 0) + b] = rec.astype(jnp.bfloat16)
             energy = jnp.sum(rec * rec, keepdims=True) * (1.0 / (NP * NS))
             energies = jnp.where(lane8 == ENERGY + s * BEAMS + b, jnp.broadcast_to(energy, (8, NS)), energies)
-    named = (owner[...] * 128 + block[...]).astype(jnp.float32)
+    named = (owner_v[...] * 128 + block_v[...]).astype(jnp.float32)
     mine[...] = jnp.where(lane8 >= COUNT, count[0, 0].astype(jnp.float32), energies)
     mine[:, 0:USES] = jnp.broadcast_to(named, (8, USES))
-    pl.semaphore_wait(barrier, COLS + ROWS - 2)
-
-    def at(dz, dx):
-        return lax.rem(z + dz + SIDE, SIDE) * SIDE + lax.rem(x + dx + SIDE, SIDE)
+    pl.semaphore_wait(barrier, len(beside))
 
     started = {}
 
@@ -584,6 +591,10 @@
     upward, downward = pl.when(row < ROWS - 1), pl.when(row > 0)
     upward(up.start)
     downward(down.start)
+    for turn in range(3):
+        for there in beside:
+            pl.semaphore_signal(met.at[turn], inc=1, device_id=there, device_id_type=MESH)
+        pl.semaphore_wait(met.at[turn], len(beside))
     downward(up.wait_recv)
     upward(down.wait_recv)
     kind8 = lax.rem(lane8, 5 * BEAMS) // BEAMS
@@ -621,11 +632,11 @@
         alarm.start()
         alarms.append(alarm)
 
-    pass_on(0)
     for route in both:
         for step in ways:
             started["b", route, step].wait_recv()
     along_second(2)
+    pass_on(0)
     to_smem.wait()
     for copy in loads:
         copy.wait()
@@ -786,7 +797,7 @@
     return pl.pallas_call(
         fused_kernel,
         out_shape=(jax.ShapeDtypeStruct((1, 1, NS), f32), jax.ShapeDtypeStruct((1,), jnp.int32)),
-        in_specs=[vmem, vmem, vmem, smem, hbm, hbm],
+        in_specs=[hbm, hbm, hbm, smem, hbm, hbm],
         out_specs=(vmem, smem),
         scratch_shapes=[
             pltpu.VMEM(((SHOTS * NP + 1) * BEAMS, NS), f32),
@@ -807,7 +818,11 @@
             pltpu.VMEM((COLS, 8, NS), f32),
             pltpu.VMEM((8, NS), f32),
             pltpu.VMEM((2, 8, NS), f32),
-            dma((3,)),
+            pltpu.VMEM(records.shape, records.dtype),
+            pltpu.VMEM(owner.shape, jnp.int32),
+            pltpu.VMEM(block.shape, jnp.int32),
+            pltpu.SemaphoreType.REGULAR((3,)),
+            dma((6,)),
             dma((COPIES,)),
             dma((COPIES,)),
             dma((2,)),

time: 47.7 us -> 45.4 us (0.952)
  Pallas kernels: 45.6 us -> 43.4 us
    pallas_call x1, Pallas kernels: 45.6 us -> 43.4 us  [fused(): pl.pallas_call(fused_kernel, out_shape=(jax.ShapeDtypeStruct((1, 1, NS),...]
where the time goes in v6:
time: 45.4 us; the launch traced here: 45.3 us
  Pallas kernels  43.4 us (96%)
  between operations  1.35 us (3%)
  local copies, waits for them, and re-layouts  0.53 us (1%)
    pallas_call x1, Pallas kernels, fused(): pl.pallas_call(fused_kernel, out_shape=(jax.ShapeDtypeStruct((1, 1, NS),...  43.4 us

profile of v6, /device:TPU:1, one launch (start us, length us, event | category | flops | bytes accessed | tf_op | source)
XLA Modules:
  0.0 45.3 jit_solution(15480391310319028088)
XLA Ops:
  0.7 0.0 copy-start.1
  0.7 0.0 copy-start.2
  0.7 0.0 copy-start.3
  0.7 43.4 %migrate.1 = (f32[1,1,128]{2,1,0:T(1,128)S(1)}, s32[1]{0:T(128)}) custom-call(bf16[2,64,8,128]{3,2,1,0:T(8,128)(2,1)} %bitcast.18, s32[1,80]{1,0:T(1,128)} %bitcast.21, s32[1,80]{1,0:T(1,128)} %bitcast.22, s32[1,1]{1,0:T(1,128)S(6)} %copy.17.count, f32[128,64,128]{2,1,0:T(8,128)} %travel.1, f32[128,64,128]{2,1,0:T(8,128)} %amp.1), custom_call_target="tpu_custom_call" | custom-call | flops 10000000 | bytes 16000000 | tf_op jit(solution)/shard_map/migrate/pallas_call | solution.py:797
  44.7 0.0 copy-done.1
  44.7 0.0 copy-done.2
  44.8 0.0 copy-done.3
  44.8 0.5 %copy.18 = f32[1,1,128]{2,1,0:T(1,128)} copy(f32[1,1,128]{2,1,0:T(1,128)S(1)} %get-tuple-element.36) | data formatting | bytes 1024
  (1 shorter events, 0.0 us)
Async XLA Ops:
  0.7 44.1 %copy-start.1 = (bf16[2,1,1,8,8192]{4,3,2,1,0:T(8,128)(2,1)S(1)}, bf16[2,1,1,8,8192]{4,3,2,1,0:T(8,128)(2,1)}, u32[]{:S(2)}) copy-start(bf16[2,1,1,8,8192]{4,3,2,1,0:T(8,128)(2,1)} %param.8) | copy-start | bytes 786436
  0.7 44.1 %copy-start.2 = (s32[80,1]{0,1:T(1,128)S(1)}, s32[80,1]{0,1:T(1,128)}, u32[]{:S(2)}) copy-start(s32[80,1]{0,1:T(1,128)} %param.10) | copy-start | bytes 964
  0.7 44.1 %copy-start.3 = (s32[80,1]{0,1:T(1,128)S(1)}, s32[80,1]{0,1:T(1,128)}, u32[]{:S(2)}) copy-start(s32[80,1]{0,1:T(1,128)} %param.11) | copy-start | bytes 964

commit v7 on v6

--- a/solution.py
+++ b/solution.py
@@ -431,6 +431,10 @@
     (((2, 2),), 24, 216, 16),
 )
 WHERE = {tile: (c, n) for c, (tiles, _, _, _) in enumerate(CLASSES) for n, tile in enumerate(tiles)}
+FAR_FIRST = sorted(
+    ((dz, dx) for dz in (0, 1, -1, 2) for dx in (0, 1, -1, 2) if (dz, dx) != (0, 0)),
+    key=lambda step: -abs(step[0]) - abs(step[1]),
+)
 SLOTS = 256
 NBLOCKS = 128
 COPIES = 40
@@ -448,7 +452,7 @@
     con0, con1, con2, con3, con4, lit0, lit1, lit2, lit3, lit4,
     flag_mine, flags, sums, parts, edge, edges, records_v, owner_v, block_v, met,
     local_sems, send_sems, recv_sems, near_send, near_recv, line_send, line_recv,
-    flag_send, flag_recv, part_send, part_recv, edge_send, edge_recv,
+    flag_send, flag_recv, part_send, part_recv, edge_send, edge_recv, late, late_in, late_send, late_recv,
 ):
     row, col = lax.axis_index("inline"), lax.axis_index("xline")
     z, x = col // SIDE, lax.rem(col, SIDE)
@@ -656,24 +660,38 @@
     arrived(1)
     arrived(-1)
     image_some(3, 0, 32)
-    early += total_of(3, listed, energy)
+    sums[...] = (early + total_of(3, listed, energy)).reshape(COLS, 8, NS)
+
+    pieces = []
+    for n, (dz, dx) in enumerate(FAR_FIRST):
+        there = at(dz, dx)
+        piece = pltpu.make_async_remote_copy(
+            sums.at[there], parts.at[n], part_send.at[n], part_recv.at[n],
+            device_id=(row, there), device_id_type=MESH,
+        )
+        piece.start()
+        pieces.append(piece)
+
     arrived(2)
     image_some(4, 0, 24)
-    sums[...] = (early + total_of(4, listed, energy)).reshape(COLS, 8, NS)
-
-    pieces = []
-    for other in range(1, COLS):
-        there = lax.rem(col + other, COLS)
-        piece = pltpu.make_async_remote_copy(
-            sums.at[there], parts.at[other], part_send.at[other], part_recv.at[other],
-            device_id=(row, there), device_id_type=MESH,
-        )
-        piece.start()
-        pieces.append(piece)
+    late[...] = total_of(4, listed, energy).reshape(COLS, 8, NS)
+    across = at(2, 2)
+    next_col, prev_col = lax.rem(across + 1, COLS), lax.rem(across + COLS - 1, COLS)
+    next_row, prev_row = lax.rem(row + 1, ROWS), lax.rem(row + ROWS - 1, ROWS)
+    direct = []
+    for n, (there_row, there_col) in enumerate(
+        ((row, across), (row, next_col), (row, prev_col), (next_row, across), (prev_row, across))
+    ):
+        copy = pltpu.make_async_remote_copy(
+            late.at[there_col], late_in.at[n], late_send.at[n], late_recv.at[n],
+            device_id=(there_row, there_col), device_id_type=MESH,
+        )
+        copy.start()
+        direct.append(copy)
     whole = sums[col]
-    for piece, other in zip(pieces, range(1, COLS)):
+    for n, piece in enumerate(pieces):
         piece.wait_recv()
-        whole += parts[other]
+        whole += parts[n]
     edge[...] = whole
     to_next = pltpu.make_async_remote_copy(
         edge, edges.at[0], edge_send.at[0], edge_recv.at[0], device_id=(row + 1, col), device_id_type=MESH
@@ -685,14 +703,19 @@
     downward(to_prev.start)
     for copy in started.values():
         copy.wait_send()
-    for copy in shares + alarms + pieces:
+    for copy in shares + alarms + pieces + direct:
         copy.wait_send()
+    for copy in direct:
+        copy.wait_recv()
+    straight = late_in[0] + late_in[1] + late_in[2]
+    contrib = whole[1:2] + straight[1:2] + late_in[3][2:3] + late_in[4][0:1]
+    lighting = whole[5:6] + straight[5:6] + late_in[3][6:7] + late_in[4][4:5]
     upward(up.wait_send)
     downward(down.wait_send)
     downward(to_next.wait_recv)
     upward(to_prev.wait_recv)
-    contrib = whole[1:2] + edges[0][2:3] + edges[1][0:1]
-    lighting = whole[5:6] + edges[0][6:7] + edges[1][4:5]
+    contrib += edges[0][2:3] + edges[1][0:1]
+    lighting += edges[0][6:7] + edges[1][4:5]
     out[0] = contrib / jnp.sqrt(1.0 + lighting)
     upward(to_next.wait_send)
     downward(to_prev.wait_send)
@@ -835,6 +858,10 @@
             dma((COLS,)),
             dma((2,)),
             dma((2,)),
+            pltpu.VMEM((COLS, 8, NS), f32),
+            pltpu.VMEM((5, 8, NS), f32),
+            dma((5,)),
+            dma((5,)),
         ],
         compiler_params=pltpu.CompilerParams(
             collective_id=0, has_side_effects=True, vmem_limit_bytes=40 << 20

time: 45.4 us -> 43.9 us (0.967)
  Pallas kernels: 43.4 us -> 41.9 us
    pallas_call x1, Pallas kernels: 43.4 us -> 41.9 us  [fused(): pl.pallas_call(fused_kernel, out_shape=(jax.ShapeDtypeStruct((1, 1, NS),...]
where the time goes in v7:
time: 43.9 us; the launch traced here: 43.8 us
  Pallas kernels  41.9 us (95%)
  between operations  1.35 us (3%)
  local copies, waits for them, and re-layouts  0.53 us (1%)
    pallas_call x1, Pallas kernels, fused(): pl.pallas_call(fused_kernel, out_shape=(jax.ShapeDtypeStruct((1, 1, NS),...  41.9 us

profile of v7, /device:TPU:1, one launch (start us, length us, event | category | flops | bytes accessed | tf_op | source)
XLA Modules:
  0.0 43.8 jit_solution(1092456007097561767)
XLA Ops:
  0.7 0.0 copy-start.1
  0.7 0.0 copy-start.2
  0.7 0.0 copy-start.3
  0.7 41.9 %migrate.1 = (f32[1,1,128]{2,1,0:T(1,128)S(1)}, s32[1]{0:T(128)}) custom-call(bf16[2,64,8,128]{3,2,1,0:T(8,128)(2,1)} %bitcast.18, s32[1,80]{1,0:T(1,128)} %bitcast.21, s32[1,80]{1,0:T(1,128)} %bitcast.22, s32[1,1]{1,0:T(1,128)S(6)} %copy.17.count, f32[128,64,128]{2,1,0:T(8,128)} %travel.1, f32[128,64,128]{2,1,0:T(8,128)} %amp.1), custom_call_target="tpu_custom_call" | custom-call | flops 10000000 | bytes 16000000 | tf_op jit(solution)/shard_map/migrate/pallas_call | solution.py:820
  43.2 0.0 copy-done.1
  43.2 0.0 copy-done.2
  43.3 0.0 copy-done.3
  43.3 0.5 %copy.18 = f32[1,1,128]{2,1,0:T(1,128)} copy(f32[1,1,128]{2,1,0:T(1,128)S(1)} %get-tuple-element.36) | data formatting | bytes 1024
  (1 shorter events, 0.0 us)
Async XLA Ops:
  0.7 42.6 %copy-start.1 = (bf16[2,1,1,8,8192]{4,3,2,1,0:T(8,128)(2,1)S(1)}, bf16[2,1,1,8,8192]{4,3,2,1,0:T(8,128)(2,1)}, u32[]{:S(2)}) copy-start(bf16[2,1,1,8,8192]{4,3,2,1,0:T(8,128)(2,1)} %param.8) | copy-start | bytes 786436
  0.7 42.6 %copy-start.2 = (s32[80,1]{0,1:T(1,128)S(1)}, s32[80,1]{0,1:T(1,128)}, u32[]{:S(2)}) copy-start(s32[80,1]{0,1:T(1,128)} %param.10) | copy-start | bytes 964
  0.7 42.6 %copy-start.3 = (s32[80,1]{0,1:T(1,128)S(1)}, s32[80,1]{0,1:T(1,128)}, u32[]{:S(2)}) copy-start(s32[80,1]{0,1:T(1,128)} %param.11) | copy-start | bytes 964

commit v8 on v6

--- a/solution.py
+++ b/solution.py
@@ -424,13 +424,17 @@
 
 
 CLASSES = (
-    (((0, 0), (1, 0), (-1, 0), (2, 0)), 56, 0, 64),
-    (((0, 1), (0, -1), (1, 1), (1, -1), (-1, 1), (-1, -1)), 80, 64, 128),
+    (((0, 0), (1, 0), (-1, 0), (2, 0)), 48, 0, 64),
+    (((0, 1), (0, -1), (1, 1), (1, -1), (-1, 1), (-1, -1)), 64, 64, 128),
     (((2, 1), (2, -1), (0, 2)), 40, 144, 64),
     (((1, 2), (-1, 2)), 32, 184, 32),
     (((2, 2),), 24, 216, 16),
 )
 WHERE = {tile: (c, n) for c, (tiles, _, _, _) in enumerate(CLASSES) for n, tile in enumerate(tiles)}
+FAR_FIRST = sorted(
+    ((dz, dx) for dz in (0, 1, -1, 2) for dx in (0, 1, -1, 2) if (dz, dx) != (0, 0)),
+    key=lambda step: -abs(step[0]) - abs(step[1]),
+)
 SLOTS = 256
 NBLOCKS = 128
 COPIES = 40
@@ -446,9 +450,10 @@
     wide, buf0, buf1, buf2, buf3, buf4, travel_v, amp_v,
     mine, near, mixed, lines, uses_v, uses_s,
     con0, con1, con2, con3, con4, lit0, lit1, lit2, lit3, lit4,
-    flag_mine, flags, sums, parts, edge, edges, records_v, owner_v, block_v, met,
+    flag_mine, flags, sums, parts, edges, records_v, owner_v, block_v, met,
     local_sems, send_sems, recv_sems, near_send, near_recv, line_send, line_recv,
     flag_send, flag_recv, part_send, part_recv, edge_send, edge_recv,
+    early_v, late_v, last_v, late_in, late_send, late_recv,
 ):
     row, col = lax.axis_index("inline"), lax.axis_index("xline")
     z, x = col // SIDE, lax.rem(col, SIDE)
@@ -640,14 +645,24 @@
     to_smem.wait()
     for copy in loads:
         copy.wait()
-    image_some(0, 0, 56)
+    image_some(0, 0, 48)
     pass_on(1)
     pass_on(-1)
-    image_some(1, 0, 80)
+    image_some(1, 0, 64)
     pass_on(2)
+    early = total_of(0, listed, energy) + total_of(1, listed, energy)
     arrived(0)
     image_some(2, 0, 40)
-    early = total_of(0, listed, energy) + total_of(1, listed, energy) + total_of(2, listed, energy)
+    early += total_of(2, listed, energy)
+    early_v[...] = early.reshape(COLS, 8, NS)
+    to_next = pltpu.make_async_remote_copy(
+        early_v, edges.at[0], edge_send.at[0], edge_recv.at[0], device_id=(row + 1, col), device_id_type=MESH
+    )
+    to_prev = pltpu.make_async_remote_copy(
+        early_v, edges.at[1], edge_send.at[1], edge_recv.at[1], device_id=(row - 1, col), device_id_type=MESH
+    )
+    upward(to_next.start)
+    downward(to_prev.start)
     raised = flag_mine[...]
     for alarm, other in zip(alarms, range(1, ROWS)):
         alarm.wait_recv()
@@ -656,46 +671,61 @@
     arrived(1)
     arrived(-1)
     image_some(3, 0, 32)
-    early += total_of(3, listed, energy)
+    late_v[...] = total_of(3, listed, energy).reshape(COLS, 8, NS)
+    next_row, prev_row = lax.rem(row + 1, ROWS), lax.rem(row + ROWS - 1, ROWS)
+    direct = []
+
+    def straight(source, dz, dx):
+        for beside_row in (next_row, prev_row):
+            n = len(direct)
+            copy = pltpu.make_async_remote_copy(
+                source.at[at(dz, dx)], late_in.at[n], late_send.at[n], late_recv.at[n],
+                device_id=(beside_row, at(dz, dx)), device_id_type=MESH,
+            )
+            copy.start()
+            direct.append(copy)
+
+    for dz, dx in ((2, 1), (2, -1), (1, 2), (-1, 2)):
+        straight(late_v, dz, dx)
     arrived(2)
     image_some(4, 0, 24)
-    sums[...] = (early + total_of(4, listed, energy)).reshape(COLS, 8, NS)
+    last_v[...] = total_of(4, listed, energy).reshape(COLS, 8, NS)
+    straight(last_v, 2, 2)
+    downward(to_next.wait_recv)
+    upward(to_prev.wait_recv)
+    own = early_v[...] + late_v[...] + last_v[...]
+    sums[...] = own + pltpu.roll(edges[0], 7, 1) + pltpu.roll(edges[1], 1, 1)
 
     pieces = []
-    for other in range(1, COLS):
-        there = lax.rem(col + other, COLS)
+    for n, (dz, dx) in enumerate(FAR_FIRST):
+        there = at(dz, dx)
         piece = pltpu.make_async_remote_copy(
-            sums.at[there], parts.at[other], part_send.at[other], part_recv.at[other],
+            sums.at[there], parts.at[n], part_send.at[n], part_recv.at[n],
             device_id=(row, there), device_id_type=MESH,
         )
         piece.start()
         pieces.append(piece)
-    whole = sums[col]
-    for piece, other in zip(pieces, range(1, COLS)):
-        piece.wait_recv()
-        whole += parts[other]
-    edge[...] = whole
-    to_next = pltpu.make_async_remote_copy(
-        edge, edges.at[0], edge_send.at[0], edge_recv.at[0], device_id=(row + 1, col), device_id_type=MESH
-    )
-    to_prev = pltpu.make_async_remote_copy(
-        edge, edges.at[1], edge_send.at[1], edge_recv.at[1], device_id=(row - 1, col), device_id_type=MESH
-    )
-    upward(to_next.start)
-    downward(to_prev.start)
     for copy in started.values():
         copy.wait_send()
-    for copy in shares + alarms + pieces:
+    for copy in shares + alarms + direct:
         copy.wait_send()
     upward(up.wait_send)
     downward(down.wait_send)
-    downward(to_next.wait_recv)
-    upward(to_prev.wait_recv)
-    contrib = whole[1:2] + edges[0][2:3] + edges[1][0:1]
-    lighting = whole[5:6] + edges[0][6:7] + edges[1][4:5]
-    out[0] = contrib / jnp.sqrt(1.0 + lighting)
     upward(to_next.wait_send)
     downward(to_prev.wait_send)
+    contrib, lighting = sums[col][1:2], sums[col][5:6]
+    for n, copy in enumerate(direct):
+        copy.wait_recv()
+        line = 2 if n % 2 == 0 else 0
+        contrib += late_in[n][line : line + 1]
+        lighting += late_in[n][line + 4 : line + 5]
+    whole = jnp.zeros((8, NS), jnp.float32)
+    for n, piece in enumerate(pieces):
+        piece.wait_recv()
+        whole += parts[n]
+    out[0] = (contrib + whole[1:2]) / jnp.sqrt(1.0 + (lighting + whole[5:6]))
+    for piece in pieces:
+        piece.wait_send()
 
 
 def row_of(route, first, second):
@@ -816,8 +846,7 @@
             pltpu.VMEM((ROWS, 8, NS), f32),
             pltpu.VMEM((COLS, 8, NS), f32),
             pltpu.VMEM((COLS, 8, NS), f32),
-            pltpu.VMEM((8, NS), f32),
-            pltpu.VMEM((2, 8, NS), f32),
+            pltpu.VMEM((2, COLS, 8, NS), f32),
             pltpu.VMEM(records.shape, records.dtype),
             pltpu.VMEM(owner.shape, jnp.int32),
             pltpu.VMEM(block.shape, jnp.int32),
@@ -835,6 +864,12 @@
             dma((COLS,)),
             dma((2,)),
             dma((2,)),
+            pltpu.VMEM((COLS, 8, NS), f32),
+            pltpu.VMEM((COLS, 8, NS), f32),
+            pltpu.VMEM((COLS, 8, NS), f32),
+            pltpu.VMEM((10, 8, NS), f32),
+            dma((10,)),
+            dma((10,)),
         ],
         compiler_params=pltpu.CompilerParams(
             collective_id=0, has_side_effects=True, vmem_limit_bytes=40 << 20

time: 45.4 us -> 43.2 us (0.952)
  Pallas kernels: 43.4 us -> 41.3 us
    pallas_call x1, Pallas kernels: 43.4 us -> 41.3 us  [fused(): pl.pallas_call(fused_kernel, out_shape=(jax.ShapeDtypeStruct((1, 1, NS),...]
where the time goes in v8:
time: 43.2 us; the launch traced here: 43.1 us
  Pallas kernels  41.3 us (96%)
  between operations  1.35 us (3%)
  local copies, waits for them, and re-layouts  0.53 us (1%)
    pallas_call x1, Pallas kernels, fused(): pl.pallas_call(fused_kernel, out_shape=(jax.ShapeDtypeStruct((1, 1, NS),...  41.3 us

profile of v8, /device:TPU:1, one launch (start us, length us, event | category | flops | bytes accessed | tf_op | source)
XLA Modules:
  0.0 43.1 jit_solution(10896515262663702652)
XLA Ops:
  0.7 0.0 copy-start.1
  0.7 0.0 copy-start.2
  0.7 0.0 copy-start.3
  0.7 41.3 %migrate.1 = (f32[1,1,128]{2,1,0:T(1,128)S(1)}, s32[1]{0:T(128)}) custom-call(bf16[2,64,8,128]{3,2,1,0:T(8,128)(2,1)} %bitcast.18, s32[1,80]{1,0:T(1,128)} %bitcast.21, s32[1,80]{1,0:T(1,128)} %bitcast.22, s32[1,1]{1,0:T(1,128)S(6)} %copy.17.count, f32[128,64,128]{2,1,0:T(8,128)} %travel.1, f32[128,64,128]{2,1,0:T(8,128)} %amp.1), custom_call_target="tpu_custom_call" | custom-call | flops 10000000 | bytes 16000000 | tf_op jit(solution)/shard_map/migrate/pallas_call | solution.py:827
  42.6 0.0 copy-done.1
  42.6 0.0 copy-done.2
  42.6 0.0 copy-done.3
  42.6 0.5 %copy.18 = f32[1,1,128]{2,1,0:T(1,128)} copy(f32[1,1,128]{2,1,0:T(1,128)S(1)} %get-tuple-element.36) | data formatting | bytes 1024
  (1 shorter events, 0.0 us)
Async XLA Ops:
  0.7 41.9 %copy-start.1 = (bf16[2,1,1,8,8192]{4,3,2,1,0:T(8,128)(2,1)S(1)}, bf16[2,1,1,8,8192]{4,3,2,1,0:T(8,128)(2,1)}, u32[]{:S(2)}) copy-start(bf16[2,1,1,8,8192]{4,3,2,1,0:T(8,128)(2,1)} %param.8) | copy-start | bytes 786436
  0.7 41.9 %copy-start.2 = (s32[80,1]{0,1:T(1,128)S(1)}, s32[80,1]{0,1:T(1,128)}, u32[]{:S(2)}) copy-start(s32[80,1]{0,1:T(1,128)} %param.10) | copy-start | bytes 964
  0.7 41.9 %copy-start.3 = (s32[80,1]{0,1:T(1,128)S(1)}, s32[80,1]{0,1:T(1,128)}, u32[]{:S(2)}) copy-start(s32[80,1]{0,1:T(1,128)} %param.11) | copy-start | bytes 964

commit v9 on v8

--- a/solution.py
+++ b/solution.py
@@ -453,7 +453,7 @@
     flag_mine, flags, sums, parts, edges, records_v, owner_v, block_v, met,
     local_sems, send_sems, recv_sems, near_send, near_recv, line_send, line_recv,
     flag_send, flag_recv, part_send, part_recv, edge_send, edge_recv,
-    early_v, late_v, last_v, late_in, late_send, late_recv,
+    early_v, late_v, last_v, late_in, late_send, late_recv, energy_v,
 ):
     row, col = lax.axis_index("inline"), lax.axis_index("xline")
     z, x = col // SIDE, lax.rem(col, SIDE)
@@ -539,18 +539,17 @@
             for way in ways:
                 started["d", route, first, way].wait_recv()
 
-    def image_some(p, begin, end):
+    def image_some(p, begin, end, group=GROUP):
         _, slots, base, held = CLASSES[p]
         buf, con, lit = bufs[p], cons[p], lits[p]
 
         def step(i, carry):
-            places = [base + i * GROUP + d for d in range(GROUP)]
+            places = [base + i * group + d for d in range(group)]
             picked = [(uses_s[0, u] & (NBLOCKS - 1), uses_s[1, u] & (held - 1)) for u in places]
-            totals = [jnp.zeros((8, NS), jnp.float32) for _ in picked]
-            squares = [jnp.zeros((8, NS), jnp.float32) for _ in picked]
-            for q in range(NP // 8):
-                rows = pl.ds(8 * q, 8)
-                for d, (number, rec) in enumerate(picked):
+            for d, (number, rec) in enumerate(picked):
+                total, square = jnp.zeros((8, NS), jnp.float32), jnp.zeros((8, NS), jnp.float32)
+                for q in range(NP // 8):
+                    rows = pl.ds(8 * q, 8)
                     t = travel_v[number, rows, :]
                     a = amp_v[number, rows, :]
                     pair = buf[rec, pl.ds(16 * (q // 2), 16), :].astype(jnp.float32)
@@ -561,26 +560,31 @@
                     w1 = f.astype(jnp.bfloat16).astype(jnp.float32)
                     v0 = jnp.take_along_axis(r, k, axis=1, mode="promise_in_bounds")
                     v1 = jnp.take_along_axis(r, k + 1, axis=1, mode="promise_in_bounds")
-                    totals[d] += a * (v0 * w0 + v1 * w1)
-                    squares[d] += a * a
-            for d in range(GROUP):
-                con[pl.ds(i * GROUP + d, 8, stride=slots), :] = totals[d]
-                lit[pl.ds(i * GROUP + d, 8, stride=slots), :] = squares[d]
+                    total += a * (v0 * w0 + v1 * w1)
+                    square += a * a
+                con[pl.ds(i * group + d, 8, stride=slots), :] = total
+                lit[pl.ds(i * group + d, 8, stride=slots), :] = square
             return carry
 
-        lax.fori_loop(begin // GROUP, end // GROUP, step, 0)
-
-    def total_of(p, listed, energy):
+        if end - begin == group:
+            step(begin // group, 0)
+        else:
+            lax.fori_loop(begin // group, end // group, step, 0)
+
+    def total_of(p, listed):
         _, slots, base, _ = CLASSES[p]
         con = sum(cons[p][pl.ds(s * slots, slots), :] for s in range(8))
-        lit = sum(lits[p][pl.ds(s * slots, slots), :] for s in range(8))
+        lit = sum(lits[p][pl.ds(s * slots, slots), :] for s in range(8)) * energy_v[pl.ds(base, slots), :]
         target = jnp.broadcast_to(listed[2:3, base : base + slots], (NS, slots))
-        weight = jnp.broadcast_to(energy[:, base : base + slots], (NS, slots))
         line = (lax.broadcasted_iota(jnp.int32, (NS, slots), 0) + 1).astype(jnp.float32)
-        to_con = jnp.where(target == line, 1.0, 0.0)
-        to_lit = jnp.where((target + 4.0 == line) & (target > 0.0), weight, 0.0)
-        dot = lambda m, v: jnp.dot(m, v, precision=lax.Precision.HIGHEST, preferred_element_type=jnp.float32)
-        return dot(to_con, con) + dot(to_lit, lit)
+        to_tile = jnp.where(target == line, 1.0, 0.0).astype(jnp.bfloat16)
+        rest = jnp.concatenate([con, lit], axis=1)
+        total = jnp.zeros((NS, 2 * NS), jnp.float32)
+        for _ in range(3):
+            part = rest.astype(jnp.bfloat16)
+            rest = rest - part.astype(jnp.float32)
+            total += jnp.dot(to_tile, part, preferred_element_type=jnp.float32)
+        return total[:, :NS] + pltpu.roll(total[:, NS:], 4, 0)
 
     for step in ways:
         for route in both:
@@ -624,6 +628,7 @@
     for share in shares:
         share.wait_recv()
     listed, energy, over = list_uses(row, col, lines)
+    energy_v[...] = jnp.transpose(jnp.broadcast_to(energy, (NS, SLOTS)))
     uses_v[...] = listed.astype(jnp.int32)
     to_smem = pltpu.make_async_copy(uses_v, uses_s, local_sems.at[2])
     to_smem.start()
@@ -650,10 +655,10 @@
     pass_on(-1)
     image_some(1, 0, 64)
     pass_on(2)
-    early = total_of(0, listed, energy) + total_of(1, listed, energy)
+    early = total_of(0, listed) + total_of(1, listed)
     arrived(0)
     image_some(2, 0, 40)
-    early += total_of(2, listed, energy)
+    early += total_of(2, listed)
     early_v[...] = early.reshape(COLS, 8, NS)
     to_next = pltpu.make_async_remote_copy(
         early_v, edges.at[0], edge_send.at[0], edge_recv.at[0], device_id=(row + 1, col), device_id_type=MESH
@@ -670,8 +675,8 @@
     flag_out[0] = jnp.max(raised).astype(jnp.int32)
     arrived(1)
     arrived(-1)
-    image_some(3, 0, 32)
-    late_v[...] = total_of(3, listed, energy).reshape(COLS, 8, NS)
+    image_some(3, 0, 32, 32)
+    late_v[...] = total_of(3, listed).reshape(COLS, 8, NS)
     next_row, prev_row = lax.rem(row + 1, ROWS), lax.rem(row + ROWS - 1, ROWS)
     direct = []
 
@@ -688,8 +693,8 @@
     for dz, dx in ((2, 1), (2, -1), (1, 2), (-1, 2)):
         straight(late_v, dz, dx)
     arrived(2)
-    image_some(4, 0, 24)
-    last_v[...] = total_of(4, listed, energy).reshape(COLS, 8, NS)
+    image_some(4, 0, 24, 24)
+    last_v[...] = total_of(4, listed).reshape(COLS, 8, NS)
     straight(last_v, 2, 2)
     downward(to_next.wait_recv)
     upward(to_prev.wait_recv)
@@ -870,6 +875,7 @@
             pltpu.VMEM((10, 8, NS), f32),
             dma((10,)),
             dma((10,)),
+            pltpu.VMEM((SLOTS, NS), f32),
         ],
         compiler_params=pltpu.CompilerParams(
             collective_id=0, has_side_effects=True, vmem_limit_bytes=40 << 20

time: 43.2 us -> 42.5 us (0.984)
  Pallas kernels: 41.3 us -> 40.5 us
    pallas_call x1, Pallas kernels: 41.3 us -> 40.5 us  [fused(): pl.pallas_call(fused_kernel, out_shape=(jax.ShapeDtypeStruct((1, 1, NS),...]
where the time goes in v9:
time: 42.5 us; the launch traced here: 42.4 us
  Pallas kernels  40.5 us (95%)
  between operations  1.35 us (3%)
  local copies, waits for them, and re-layouts  0.53 us (1%)
    pallas_call x1, Pallas kernels, fused(): pl.pallas_call(fused_kernel, out_shape=(jax.ShapeDtypeStruct((1, 1, NS),...  40.5 us

profile of v9, /device:TPU:1, one launch (start us, length us, event | category | flops | bytes accessed | tf_op | source)
XLA Modules:
  0.0 42.4 jit_solution(4812380065979637521)
XLA Ops:
  0.7 0.0 copy-start.1
  0.7 0.0 copy-start.2
  0.7 0.0 copy-start.3
  0.7 40.5 %migrate.1 = (f32[1,1,128]{2,1,0:T(1,128)S(1)}, s32[1]{0:T(128)}) custom-call(bf16[2,64,8,128]{3,2,1,0:T(8,128)(2,1)} %bitcast.18, s32[1,80]{1,0:T(1,128)} %bitcast.21, s32[1,80]{1,0:T(1,128)} %bitcast.22, s32[1,1]{1,0:T(1,128)S(6)} %copy.17.count, f32[128,64,128]{2,1,0:T(8,128)} %travel.1, f32[128,64,128]{2,1,0:T(8,128)} %amp.1), custom_call_target="tpu_custom_call" | custom-call | flops 10000000 | bytes 16000000 | tf_op jit(solution)/shard_map/migrate/pallas_call | solution.py:832
  41.8 0.0 copy-done.1
  41.9 0.0 copy-done.2
  41.9 0.0 copy-done.3
  41.9 0.5 %copy.18 = f32[1,1,128]{2,1,0:T(1,128)} copy(f32[1,1,128]{2,1,0:T(1,128)S(1)} %get-tuple-element.36) | data formatting | bytes 1024
  (1 shorter events, 0.0 us)
Async XLA Ops:
  0.7 41.2 %copy-start.1 = (bf16[2,1,1,8,8192]{4,3,2,1,0:T(8,128)(2,1)S(1)}, bf16[2,1,1,8,8192]{4,3,2,1,0:T(8,128)(2,1)}, u32[]{:S(2)}) copy-start(bf16[2,1,1,8,8192]{4,3,2,1,0:T(8,128)(2,1)} %param.8) | copy-start | bytes 786436
  0.7 41.2 %copy-start.2 = (s32[80,1]{0,1:T(1,128)S(1)}, s32[80,1]{0,1:T(1,128)}, u32[]{:S(2)}) copy-start(s32[80,1]{0,1:T(1,128)} %param.10) | copy-start | bytes 964
  0.7 41.2 %copy-start.3 = (s32[80,1]{0,1:T(1,128)S(1)}, s32[80,1]{0,1:T(1,128)}, u32[]{:S(2)}) copy-start(s32[80,1]{0,1:T(1,128)} %param.11) | copy-start | bytes 964

commit v10 on v9

--- a/solution.py
+++ b/solution.py
@@ -600,10 +600,12 @@
     upward, downward = pl.when(row < ROWS - 1), pl.when(row > 0)
     upward(up.start)
     downward(down.start)
-    for turn in range(3):
-        for there in beside:
+    apart = [(row, at(dz, dx)) for dz, dx in ((1, 1), (1, -1), (-1, 1), (-1, -1), (0, 2), (2, 0))]
+    apart += [(lax.rem(row + 2, ROWS), col), (lax.rem(row + ROWS - 2, ROWS), col)]
+    for turn, others in enumerate((beside, apart)):
+        for there in others:
             pl.semaphore_signal(met.at[turn], inc=1, device_id=there, device_id_type=MESH)
-        pl.semaphore_wait(met.at[turn], len(beside))
+        pl.semaphore_wait(met.at[turn], len(others))
     downward(up.wait_recv)
     upward(down.wait_recv)
     kind8 = lax.rem(lane8, 5 * BEAMS) // BEAMS
@@ -650,14 +652,14 @@
     to_smem.wait()
     for copy in loads:
         copy.wait()
-    image_some(0, 0, 48)
+    image_some(0, 0, 48, 16)
     pass_on(1)
     pass_on(-1)
-    image_some(1, 0, 64)
+    image_some(1, 0, 64, 16)
     pass_on(2)
     early = total_of(0, listed) + total_of(1, listed)
     arrived(0)
-    image_some(2, 0, 40)
+    image_some(2, 0, 40, 20)
     early += total_of(2, listed)
     early_v[...] = early.reshape(COLS, 8, NS)
     to_next = pltpu.make_async_remote_copy(
@@ -855,7 +857,7 @@
             pltpu.VMEM(records.shape, records.dtype),
             pltpu.VMEM(owner.shape, jnp.int32),
             pltpu.VMEM(block.shape, jnp.int32),
-            pltpu.SemaphoreType.REGULAR((3,)),
+            pltpu.SemaphoreType.REGULAR((2,)),
             dma((6,)),
             dma((COPIES,)),
             dma((COPIES,)),

time: 42.5 us -> 42.5 us (level)
  no operation moved by 1% of the time
where the time goes in v10:
time: 42.5 us; the launch traced here: 42.4 us
  Pallas kernels  40.5 us (95%)
  between operations  1.35 us (3%)
  local copies, waits for them, and re-layouts  0.53 us (1%)
    pallas_call x1, Pallas kernels, fused(): pl.pallas_call(fused_kernel, out_shape=(jax.ShapeDtypeStruct((1, 1, NS),...  40.5 us

profile of v10, /device:TPU:1, one launch (start us, length us, event | category | flops | bytes accessed | tf_op | source)
XLA Modules:
  0.0 42.4 jit_solution(17284183510629327553)
XLA Ops:
  0.7 0.0 copy-start.1
  0.7 0.0 copy-start.2
  0.7 0.0 copy-start.3
  0.7 40.5 %migrate.1 = (f32[1,1,128]{2,1,0:T(1,128)S(1)}, s32[1]{0:T(128)}) custom-call(bf16[2,64,8,128]{3,2,1,0:T(8,128)(2,1)} %bitcast.18, s32[1,80]{1,0:T(1,128)} %bitcast.21, s32[1,80]{1,0:T(1,128)} %bitcast.22, s32[1,1]{1,0:T(1,128)S(6)} %copy.17.count, f32[128,64,128]{2,1,0:T(8,128)} %travel.1, f32[128,64,128]{2,1,0:T(8,128)} %amp.1), custom_call_target="tpu_custom_call" | custom-call | flops 10000000 | bytes 16000000 | tf_op jit(solution)/shard_map/migrate/pallas_call | solution.py:834
  41.8 0.0 copy-done.1
  41.8 0.0 copy-done.2
  41.8 0.0 copy-done.3
  41.9 0.5 %copy.18 = f32[1,1,128]{2,1,0:T(1,128)} copy(f32[1,1,128]{2,1,0:T(1,128)S(1)} %get-tuple-element.36) | data formatting | bytes 1024
  (1 shorter events, 0.0 us)
Async XLA Ops:
  0.7 41.2 %copy-start.1 = (bf16[2,1,1,8,8192]{4,3,2,1,0:T(8,128)(2,1)S(1)}, bf16[2,1,1,8,8192]{4,3,2,1,0:T(8,128)(2,1)}, u32[]{:S(2)}) copy-start(bf16[2,1,1,8,8192]{4,3,2,1,0:T(8,128)(2,1)} %param.8) | copy-start | bytes 786436
  0.7 41.2 %copy-start.2 = (s32[80,1]{0,1:T(1,128)S(1)}, s32[80,1]{0,1:T(1,128)}, u32[]{:S(2)}) copy-start(s32[80,1]{0,1:T(1,128)} %param.10) | copy-start | bytes 964
  0.7 41.2 %copy-start.3 = (s32[80,1]{0,1:T(1,128)S(1)}, s32[80,1]{0,1:T(1,128)}, u32[]{:S(2)}) copy-start(s32[80,1]{0,1:T(1,128)} %param.11) | copy-start | bytes 964

commit v11 on v10

--- a/solution.py
+++ b/solution.py
@@ -659,7 +659,7 @@
     pass_on(2)
     early = total_of(0, listed) + total_of(1, listed)
     arrived(0)
-    image_some(2, 0, 40, 20)
+    image_some(2, 0, 40, 40)
     early += total_of(2, listed)
     early_v[...] = early.reshape(COLS, 8, NS)
     to_next = pltpu.make_async_remote_copy(

time: 42.5 us -> 42.5 us (level)
  no operation moved by 1% of the time
where the time goes in v11:
time: 42.5 us; the launch traced here: 42.4 us
  Pallas kernels  40.5 us (95%)
  between operations  1.35 us (3%)
  local copies, waits for them, and re-layouts  0.53 us (1%)
    pallas_call x1, Pallas kernels, fused(): pl.pallas_call(fused_kernel, out_shape=(jax.ShapeDtypeStruct((1, 1, NS),...  40.5 us

profile of v11, /device:TPU:1, one launch (start us, length us, event | category | flops | bytes accessed | tf_op | source)
XLA Modules:
  0.0 42.4 jit_solution(10336294866784300544)
XLA Ops:
  0.7 0.0 copy-start.1
  0.7 0.0 copy-start.2
  0.7 0.0 copy-start.3
  0.7 40.5 %migrate.1 = (f32[1,1,128]{2,1,0:T(1,128)S(1)}, s32[1]{0:T(128)}) custom-call(bf16[2,64,8,128]{3,2,1,0:T(8,128)(2,1)} %bitcast.18, s32[1,80]{1,0:T(1,128)} %bitcast.21, s32[1,80]{1,0:T(1,128)} %bitcast.22, s32[1,1]{1,0:T(1,128)S(6)} %copy.17.count, f32[128,64,128]{2,1,0:T(8,128)} %travel.1, f32[128,64,128]{2,1,0:T(8,128)} %amp.1), custom_call_target="tpu_custom_call" | custom-call | flops 10000000 | bytes 16000000 | tf_op jit(solution)/shard_map/migrate/pallas_call | solution.py:834
  41.8 0.0 copy-done.1
  41.8 0.0 copy-done.2
  41.8 0.0 copy-done.3
  41.9 0.5 %copy.18 = f32[1,1,128]{2,1,0:T(1,128)} copy(f32[1,1,128]{2,1,0:T(1,128)S(1)} %get-tuple-element.36) | data formatting | bytes 1024
  (1 shorter events, 0.0 us)
Async XLA Ops:
  0.7 41.2 %copy-start.1 = (bf16[2,1,1,8,8192]{4,3,2,1,0:T(8,128)(2,1)S(1)}, bf16[2,1,1,8,8192]{4,3,2,1,0:T(8,128)(2,1)}, u32[]{:S(2)}) copy-start(bf16[2,1,1,8,8192]{4,3,2,1,0:T(8,128)(2,1)} %param.8) | copy-start | bytes 786436
  0.7 41.2 %copy-start.2 = (s32[80,1]{0,1:T(1,128)S(1)}, s32[80,1]{0,1:T(1,128)}, u32[]{:S(2)}) copy-start(s32[80,1]{0,1:T(1,128)} %param.10) | copy-start | bytes 964
  0.7 41.2 %copy-start.3 = (s32[80,1]{0,1:T(1,128)S(1)}, s32[80,1]{0,1:T(1,128)}, u32[]{:S(2)}) copy-start(s32[80,1]{0,1:T(1,128)} %param.11) | copy-start | bytes 964
